TPU v7x, 512 devices: a whole 4x8x8 slice. The times are simulated.
512 devices in a mesh: grp: 16 (over x, y_lo, core), blk: 32 (over z, y_hi).
Axes of the slice: x: 4, y: 8 (y_hi: 4, y_lo: 2; y = y_hi * 2 + y_lo), z: 8, core: 2. Of those that a mesh axis runs over, the one named last changes fastest.
Arguments:
- series: bfloat16 [32, 512, 49152], P('grp', None, 'blk')
- labels: int32 [32], replicated, may hold values from 0 to 3, as said below
- panel_owner: int32 [2], replicated, may hold values from 0 to 31
Outputs:
- connectome: bfloat16 [2, 256, 49152], P(None, 'grp', 'blk')
Inputs may be any that keep to these rules, and one draw needn't show every extreme that they name: `labels`: group 0 holds exactly one subject, group 1 exactly max(4, 1), group 2 exactly max(8, 1), group 3 the rest; which subjects is drawn.
All inputs are finite; a program needn't handle non-finite values.
Results may differ from a plain program's by a relative error of at most 0.011.
Values may be sent and summed in bfloat16 or wider, within the bound.
A program may use at most 64 MiB of HBM per device.

v0:
```python
import jax
import jax.numpy as jnp
from jax import lax
from jax.sharding import PartitionSpec as P

PANEL = 256
STEPS = 2
COHORTS = 4


epsilon = 1e-05
clip_limit = 0.99


def from_root(array, axis, root):
    mine = lax.axis_index(axis) == root
    return lax.psum(jnp.where(mine, array, jnp.zeros_like(array)), axis)


def standardize(series):
    values = series.astype(jnp.float32)
    center = jnp.mean(values, axis=1, keepdims=True)
    centred = values - center
    spread = jnp.mean(centred * centred, axis=1, keepdims=True)
    return (centred * lax.rsqrt(spread + epsilon)).astype(jnp.bfloat16)


def fisher_z(correl):
    bounded = jnp.clip(correl, -clip_limit, clip_limit)
    return 0.5 * jnp.log((1.0 + bounded) / (1.0 - bounded))


def body(series, labels, panel_owner):
    members, frames, columns = series.shape
    scored = standardize(series)
    cohort_ids = jnp.arange(COHORTS, dtype=jnp.int32)
    onehot = (labels[:, None] == cohort_ids[None, :]).astype(jnp.float32)
    counts = jnp.sum(onehot, axis=0)
    inverse = 1.0 / (COHORTS * counts)
    local_labels = lax.dynamic_slice_in_dim(labels, lax.axis_index("grp") * members, members)
    local_onehot = (local_labels[:, None] == cohort_ids[None, :]).astype(jnp.float32)
    weight = jnp.sum(local_onehot * inverse[None, :], axis=1)
    own_block = lax.axis_index("blk")
    panels = []
    for step_index in range(STEPS):
        owner = panel_owner[step_index]
        own_panel = scored[:, :, step_index * PANEL : (step_index + 1) * PANEL]
        panels.append(from_root(own_panel, "blk", owner))
    results = []
    for step_index in range(STEPS):
        upper = own_block >= panel_owner[step_index]
        correl = jnp.einsum(
            "sfp,sfc->spc", panels[step_index], scored, preferred_element_type=jnp.float32
        ) / float(frames)
        fisher = fisher_z(correl)
        partial_value = jnp.where(upper, jnp.einsum("s,spc->pc", weight, fisher), 0.0)
        results.append(
            lax.psum_scatter(partial_value, "grp", scatter_dimension=0, tiled=True).astype(
                jnp.bfloat16
            )
        )
    return jnp.stack(results)


def solution(mesh):
    in_specs = (P("grp", None, "blk"), P(), P())
    out_specs = P(None, "grp", "blk")
    return jax.shard_map(body, mesh=mesh, in_specs=in_specs, out_specs=out_specs, check_vma=False)
```

profile of v0, /device:TPU:1, one launch (start us, length us, event | category | flops | bytes accessed | tf_op | source)
XLA Modules:
  0.0 488.2 jit_solution(15715550495113765115)
XLA Ops:
  6.5 1.3 fusion.13
  9.1 3.2 copy.7
  12.3 0.5 convert_reduce_fusion
  12.8 1.3 fusion.2
  14.1 1.0 fusion.3
  15.2 1.7 copy-done
  16.8 1.0 slice_select_fusion.1
  17.9 0.0 reduce-scatter.3.cloned.1.call-start
  18.6 0.1 dynamic_slice.3
  18.7 0.1 convert_reduce_fusion.1
  18.8 0.2 fusion.10
  19.0 303.2 %all-reduce.3.cloned.1.call-done = (bf16[2,512,256]{1,2,0:T(8,128)(2,1)}, bf16[2,512,256]{1,2,0:T(8,128)(2,1)}) async-done(((bf16[2,512,256]{1,2,0:T(8,128)(2,1)}, bf16[2,512,256]{1,2,0:T(8,128)(2,1)}), (bf16[2,512,256]{1,2,0:T(8,128)(2,1)}, bf16[2,512,256]{1,2,0:T(8,128)(2,1)})) %all-reduce.3.cloned.1.call-update) | async-done | bytes 1048592 | tf_op jit(solution)/shard_map/psum | solution.py:17
  322.2 3.5 log_multiply_fusion.1
  325.6 1.8 fusion.8
  327.4 1.3 bitcast_select_fusion.1
  329.5 0.4 copy-done.1
  329.9 2.5 log_multiply_fusion
  332.3 1.8 fusion.6
  334.1 1.3 bitcast_select_fusion
  335.4 75.9 %reduce-scatter.3.cloned.1.call-done = f32[16,1536]{1,0:T(8,128)} async-done(((f32[256,1536]{1,0:T(8,128)}), f32[16,1536]{1,0:T(8,128)}) %reduce-scatter.3.cloned.1.call-update) | async-done | bytes 98320 | tf_op jit(solution)/shard_map/reduce_scatter | solution.py:58
  411.3 0.9 convert_bitcast_fusion.1
  412.2 67.9 %reduce-scatter.5.cloned.1.call-done = f32[16,1536]{1,0:T(8,128)} async-done(((f32[256,1536]{1,0:T(8,128)}), f32[16,1536]{1,0:T(8,128)}) %reduce-scatter.5.cloned.1.call-update) | async-done | bytes 98320 | tf_op jit(solution)/shard_map/reduce_scatter | solution.py:58
  480.1 0.9 convert_bitcast_fusion
  481.0 0.7 pad_maximum_fusion
  (12 shorter events, 0.1 us)
Async XLA Ops:
  6.5 315.6 %all-reduce.3.cloned.1.call-start = ((), (), s32[]{:S(2)}) async-start(), calls=%async_computation.4 | async-start | bytes 2097152 | tf_op jit(solution)/shard_map/psum | solution.py:17
  15.2 1.7 copy-start
  16.8 1.8 copy-start.2
  17.9 393.4 %reduce-scatter.3.cloned.1.call-start = ((), (), s32[]{:S(2)}) async-start(), calls=%async_computation.2 | async-start | bytes 1671168 | tf_op jit(solution)/shard_map/reduce_scatter | solution.py:58
  327.4 2.5 copy-start.1
  328.7 151.4 %reduce-scatter.5.cloned.1.call-start = ((), (), s32[]{:S(2)}) async-start(), calls=%async_computation.3 | async-start | bytes 1671168 | tf_op jit(solution)/shard_map/reduce_scatter | solution.py:58
Sparse Core Ops, SparseCore 0:
  18.0 304.1 all-reduce.2
  328.8 82.3 reduce-scatter.2
  414.1 65.9 reduce-scatter.4
where the time goes:
time: 490 us; the launch traced here: 488 us
  waiting for transfers between devices  447 us (91%)
  between operations  15.8 us (3%)
  matrix products  9.46 us (2%)
  other arithmetic  9.21 us (2%)
  local copies, waits for them, and re-layouts  6.62 us (1%)
    psum x1, waiting for transfers between devices, from_root(): return lax.psum(jnp.where(mine, array, jnp.zeros_like(array)), axis)  303 us
    reduce_scatter x2, waiting for transfers between devices, body(): lax.psum_scatter(partial_value, 'grp', scatter_dimension=0, tiled=True)  144 us
  transfers between devices with their start and end apart: 3, of which 3 were waited for; matrix products, arithmetic and copies ran while one was open for 1% of the time, Pallas kernels for 0%

commit v1 on v0

v1 whole, which is shorter than its diff:
```python
import functools

import jax
import jax.numpy as jnp
from jax import lax
from jax.experimental import pallas as pl
from jax.experimental.pallas import tpu as pltpu
from jax.sharding import PartitionSpec as P

MESH = pl.DeviceIdType.MESH
STEPS, PANEL, COHORTS, MEMBERS = 2, 256, 4, 2
FRAMES, COLUMNS = 512, 1536
NZ, NY, NQ, NC = 8, 4, 8, 2
N_GRP, N_BLK = NQ * NC, NZ * NY
CHUNK = MEMBERS * PANEL // NZ
PIECE = CHUNK // NY
OUT_ROWS = PANEL // N_GRP
TILE = 256
ROWS = 128
epsilon = 1e-05
clip_limit = 0.99

N_COPIES = STEPS * (7 + 6 + 7 + 1 + 7)


def kernel(
    labels_ref, owner_ref, series_ref, out_ref,
    raw, scored, panel, land_a, mid, land_b, whole, part, land_e, half, land_h,
    load_sem, send_sem, recv_sem,
):
    grp, blk = lax.axis_index("grp"), lax.axis_index("blk")
    zi, yi = blk // NY, blk % NY
    qi, core = grp // NC, grp % NC

    def at_z(offset):
        return {"blk": ((zi + offset + NZ) % NZ) * NY + yi}

    def at_y(offset):
        return {"blk": zi * NY + (yi + offset) % NY}

    def at_q(offset):
        return {"grp": ((qi + offset) % NQ) * NC + core}

    other_core = {"grp": qi * NC + 1 - core}

    loads = []
    for k, (start, width) in enumerate(
        [(0, PANEL), (PANEL, PANEL), (STEPS * PANEL, COLUMNS - STEPS * PANEL)]
    ):
        window = (slice(None), slice(None), pl.ds(start, width))
        loads.append(
            pltpu.make_async_copy(series_ref.at[window], raw.at[window], load_sem.at[k])
        )
        loads[-1].start()

    barrier = pltpu.get_barrier_semaphore()
    peers = [at_z(1), at_z(-1)]
    peers += [at_y(o) for o in range(1, NY)]
    peers += [other_core]
    peers += [at_q(o) for o in range(1, NQ)]
    for peer in peers:
        pl.semaphore_signal(barrier, inc=1, device_id=peer, device_id_type=MESH)

    count = [0]

    def send(src, dst, device):
        k = count[0]
        count[0] += 1
        copy = pltpu.make_async_remote_copy(
            src_ref=src,
            dst_ref=dst,
            send_sem=send_sem.at[k],
            recv_sem=recv_sem.at[k],
            device_id=device,
            device_id_type=MESH,
        )
        copy.start()
        return copy

    started = []

    def standardize(s, start, step):
        cols = pl.ds(start, TILE)
        total = jnp.zeros((8, TILE), jnp.float32)
        for r in range(0, FRAMES, ROWS):
            x = raw[s, pl.ds(r, ROWS), cols].astype(jnp.float32)
            total += jnp.sum(x.reshape(ROWS // 8, 8, TILE), axis=0)
        center = jnp.sum(total, axis=0, keepdims=True) * (1.0 / FRAMES)
        total = jnp.zeros((8, TILE), jnp.float32)
        for r in range(0, FRAMES, ROWS):
            x = raw[s, pl.ds(r, ROWS), cols].astype(jnp.float32) - center
            total += jnp.sum((x * x).reshape(ROWS // 8, 8, TILE), axis=0)
        spread = jnp.sum(total, axis=0, keepdims=True) * (1.0 / FRAMES)
        scale = lax.rsqrt(spread + epsilon)
        for r in range(0, FRAMES, ROWS):
            x = raw[s, pl.ds(r, ROWS), cols].astype(jnp.float32) - center
            y = x * scale
            scored[s, pl.ds(r, ROWS), cols] = y.astype(jnp.bfloat16)
            if step is not None:
                mine = jnp.where(owner_ref[step] == blk, 1.0, 0.0)
                turned = (y * mine).T.astype(jnp.bfloat16)
                per = PANEL // CHUNK
                panel[step, pl.ds(s * per, per), :, pl.ds(r, ROWS)] = turned.reshape(
                    per, CHUNK, ROWS
                )

    rest = [
        (s, c) for s in range(MEMBERS) for c in range(STEPS * PANEL, COLUMNS, TILE)
    ]

    def some_rest(n):
        for _ in range(n):
            if rest:
                standardize(*rest.pop(0), None)

    def hops(k, sign):
        return 4 if (sign > 0) == (k == 0) else 3

    a_copies = {}

    def send_a(k, sign, t):
        reach = hops(k, sign)
        d = (zi + sign * (reach - t) + NZ) % NZ
        way = 0 if sign > 0 else 1
        if t == 0:
            src = panel.at[k, d]
        else:
            a_copies[k, sign, t - 1].wait_recv()
            src = land_a.at[k, way, t - 1]
            src[...] += panel[k, d]
        a_copies[k, sign, t] = send(src, land_a.at[k, way, t], at_z(sign))

    for k in range(STEPS):
        loads[k].wait()
        for s in range(MEMBERS):
            standardize(s, k * PANEL, k)
        if k == 0:
            pl.semaphore_wait(barrier, len(peers))
        for sign in (1, -1):
            send_a(k, sign, 0)
    loads[2].wait()
    for t in range(1, 4):
        some_rest(2)
        for k in range(STEPS):
            for sign in (1, -1):
                if t < hops(k, sign):
                    send_a(k, sign, t)
    some_rest(2)

    b_copies = {}
    for k in range(STEPS):
        for sign in (1, -1):
            a_copies[k, sign, hops(k, sign) - 1].wait_recv()
        got = [land_a[k, w, hops(k, sign) - 1] for w, sign in ((0, 1), (1, -1))]
        mid[k] = (panel[k, zi] + got[0] + got[1]).reshape(NY, PIECE, FRAMES)
        for o in (2, 1, 3):
            b_copies[k, o] = send(
                mid.at[k, (yi + o) % NY], land_b.at[k, o - 1], at_y(o)
            )
    g_copies = {}
    for k in range(STEPS):
        for o in range(1, NY):
            b_copies[k, o].wait_recv()
        whole[k, zi, yi] = mid[k, yi] + land_b[k, 0] + land_b[k, 1] + land_b[k, 2]
        for o in (2, 1, 3):
            g_copies[k, o] = send(
                whole.at[k, zi, yi], whole.at[k, zi, yi], at_y(o)
            )
    some_rest(8)

    c_copies = {}

    def send_c(k, sign, t):
        if t:
            c_copies[k, sign, t - 1].wait_recv()
        d = (zi - sign * t + NZ) % NZ
        c_copies[k, sign, t] = send(whole.at[k, d], whole.at[k, d], at_z(sign))

    for k in range(STEPS):
        for o in range(1, NY):
            g_copies[k, o].wait_recv()
        for sign in (1, -1):
            send_c(k, sign, 0)
    for t in range(1, 4):
        for k in range(STEPS):
            for sign in (1, -1):
                if t < hops(k, sign):
                    send_c(k, sign, t)

    halves = []
    for s in range(MEMBERS):
        label = labels_ref[grp * MEMBERS + s]
        same = jnp.int32(0)
        for i in range(N_GRP * MEMBERS):
            same += jnp.where(labels_ref[i] == label, 1, 0)
        counted = jnp.full((1, TILE), same.astype(jnp.float32))
        halves.append(0.5 / (COHORTS * counted))

    d_copies = {}
    for k in range(STEPS):
        for sign in (1, -1):
            c_copies[k, sign, hops(k, sign) - 1].wait_recv()

        def tile(j, carry, k=k):
            cols = pl.ds(pl.multiple_of(j * TILE, TILE), TILE)
            total = None
            per = NZ // MEMBERS
            for s in range(MEMBERS):
                rows = whole[k, pl.ds(s * per, per)].reshape(PANEL, FRAMES)
                q = jnp.dot(
                    rows, scored[s, :, cols], preferred_element_type=jnp.float32
                ) * (1.0 / FRAMES)
                q = jnp.clip(q, -clip_limit, clip_limit)
                term = halves[s] * jnp.log((1.0 + q) / (1.0 - q))
                total = term if total is None else total + term
            part[k, :, :, :, cols] = total.astype(jnp.bfloat16).reshape(
                NQ, NC, OUT_ROWS, TILE
            )
            return carry

        lax.fori_loop(0, COLUMNS // TILE, tile, 0)
        d_copies[k] = send(part.at[k, :, 1 - core], land_e.at[k], other_core)

    h_copies = {}
    for k in range(STEPS):
        d_copies[k].wait_recv()
        half[k] = (
            part[k, :, core].astype(jnp.float32) + land_e[k].astype(jnp.float32)
        ).astype(jnp.bfloat16)
        for o in (4, 3, 5, 2, 6, 1, 7):
            h_copies[k, o] = send(
                half.at[k, (qi + o) % NQ], land_h.at[k, o - 1], at_q(o)
            )
    for k in range(STEPS):
        total = half[k, qi].astype(jnp.float32)
        for o in range(1, NQ):
            h_copies[k, o].wait_recv()
            total += land_h[k, o - 1].astype(jnp.float32)
        out_ref[k] = total

    for copies in (a_copies, b_copies, g_copies, c_copies, d_copies, h_copies):
        for copy in copies.values():
            copy.wait_send()


def body(series, labels, panel_owner):
    half_type = jnp.bfloat16
    summed = pl.pallas_call(
        kernel,
        out_shape=jax.ShapeDtypeStruct((STEPS, OUT_ROWS, COLUMNS), jnp.float32),
        in_specs=[
            pl.BlockSpec(memory_space=pltpu.SMEM),
            pl.BlockSpec(memory_space=pltpu.SMEM),
            pl.BlockSpec(memory_space=pl.ANY),
        ],
        out_specs=pl.BlockSpec(memory_space=pltpu.VMEM),
        scratch_shapes=[
            pltpu.VMEM((MEMBERS, FRAMES, COLUMNS), half_type),
            pltpu.VMEM((MEMBERS, FRAMES, COLUMNS), half_type),
            pltpu.VMEM((STEPS, NZ, CHUNK, FRAMES), half_type),
            pltpu.VMEM((STEPS, 2, 4, CHUNK, FRAMES), half_type),
            pltpu.VMEM((STEPS, NY, PIECE, FRAMES), half_type),
            pltpu.VMEM((STEPS, NY - 1, PIECE, FRAMES), half_type),
            pltpu.VMEM((STEPS, NZ, NY, PIECE, FRAMES), half_type),
            pltpu.VMEM((STEPS, NQ, NC, OUT_ROWS, COLUMNS), half_type),
            pltpu.VMEM((STEPS, NQ, OUT_ROWS, COLUMNS), half_type),
            pltpu.VMEM((STEPS, NQ, OUT_ROWS, COLUMNS), half_type),
            pltpu.VMEM((STEPS, NQ - 1, OUT_ROWS, COLUMNS), half_type),
            pltpu.SemaphoreType.DMA((3,)),
            pltpu.SemaphoreType.DMA((N_COPIES,)),
            pltpu.SemaphoreType.DMA((N_COPIES,)),
        ],
        compiler_params=pltpu.CompilerParams(
            collective_id=0, has_side_effects=True, vmem_limit_bytes=40 * 1024 * 1024
        ),
    )(labels, panel_owner, series)
    upper = lax.axis_index("blk") >= panel_owner
    return jnp.where(upper[:, None, None], summed, 0.0).astype(jnp.bfloat16)


def solution(mesh):
    in_specs = (P("grp", None, "blk"), P(), P())
    out_specs = P(None, "grp", "blk")
    return jax.shard_map(body, mesh=mesh, in_specs=in_specs, out_specs=out_specs, check_vma=False)
```

time: 490 us -> 75.6 us (0.15)
  waiting for transfers between devices: 447 us -> 0 us
  Pallas kernels: 0 us -> 70.8 us
  between operations: 15.8 us -> 0.01 us
  matrix products: 9.46 us -> 0 us
  other arithmetic: 9.21 us -> 1.38 us
    psum x1 -> x0, waiting for transfers between devices: 303 us -> none  [from_root(): return lax.psum(jnp.where(mine, array, jnp.zeros_like(array)), axis)]
    reduce_scatter x2 -> x0, waiting for transfers between devices: 144 us -> none  [body(): lax.psum_scatter(partial_value, 'grp', scatter_dimension=0, tiled=True)]
    pallas_call x0 -> x1, Pallas kernels: none -> 70.8 us  [body(): pl.pallas_call(kernel, out_shape=jax.ShapeDtypeStruct((STEPS, OUT_ROWS, C...]
    dot_general x4 -> x0, matrix products: 9.46 us -> none  [the longest x2 5.92 us: body(): jnp.einsum('sfp,sfc->spc', panels[step_index], scored, preferred_element_...]
  transfers between devices with their start and end apart: 3 -> 0, of which waited for: 3 -> 0; matrix products, arithmetic and copies ran while one was open for 1% -> 0% of each run, Pallas kernels for 0% -> 0%
where the time goes in v1:
time: 75.6 us; the launch traced here: 75.4 us
  Pallas kernels  70.8 us (94%)
  local copies, waits for them, and re-layouts  3.2 us (4%)
  other arithmetic  1.38 us (2%)
    pallas_call x1, Pallas kernels, body(): pl.pallas_call(kernel, out_shape=jax.ShapeDtypeStruct((STEPS, OUT_ROWS, C...  70.8 us
    unnamed x6, local copies, waits for them, and re-layouts  3.2 us

profile of v1, /device:TPU:1, one launch (start us, length us, event | category | flops | bytes accessed | tf_op | source)
XLA Modules:
  0.0 75.4 jit_solution(6893716823208687771)
XLA Ops:
  0.0 0.7 broadcast_compare_fusion
  0.7 0.0 copy-start
  0.7 1.9 %copy-done = bf16[2,512,1536]{2,1,0:T(8,128)(2,1)S(1)} copy-done((bf16[2,512,1536]{2,1,0:T(8,128)(2,1)S(1)}, bf16[2,512,1536]{2,1,0:T(8,128)(2,1)}, u32[]{:S(2)}) %copy-start) | copy-done | bytes 3145752
  2.6 0.0 copy-start.1
  2.6 0.7 copy-done.1
  3.2 0.0 copy-start.2
  3.2 0.7 copy-done.2
  3.9 70.8 %shard_map.37 = f32[2,16,1536]{2,1,0:T(8,128)S(1)} custom-call(s32[32]{0:T(128)S(1)} %copy-done.1, s32[2]{0:T(128)S(1)} %copy-done.2, bf16[2,512,1536]{2,1,0:T(8,128)(2,1)S(1)} %copy-done), custom_call_target="tpu_custom_call" | custom-call | tf_op jit(solution)/shard_map/pallas_call | solution.py:248
  74.7 0.7 select_convert_fusion
Async XLA Ops:
  0.7 1.9 %copy-start = (bf16[2,512,1536]{2,1,0:T(8,128)(2,1)S(1)}, bf16[2,512,1536]{2,1,0:T(8,128)(2,1)}, u32[]{:S(2)}) copy-start(bf16[2,512,1536]{2,1,0:T(8,128)(2,1)} %series_ref.1) | copy-start | bytes 9437188
  2.6 0.7 copy-start.1
  3.2 0.7 copy-start.2

commit v2 on v1

--- a/solution.py
+++ b/solution.py
@@ -14,19 +14,20 @@
 N_GRP, N_BLK = NQ * NC, NZ * NY
 CHUNK = MEMBERS * PANEL // NZ
 PIECE = CHUNK // NY
+SHARE = PANEL // NZ
 OUT_ROWS = PANEL // N_GRP
 TILE = 256
 ROWS = 128
 epsilon = 1e-05
 clip_limit = 0.99
 
-N_COPIES = STEPS * (7 + 6 + 7 + 1 + 7)
+N_COPIES = STEPS * (7 + 6 + 7) + NQ + NQ - 1
 
 
 def kernel(
-    labels_ref, owner_ref, series_ref, out_ref,
-    raw, scored, panel, land_a, mid, land_b, whole, part, land_e, half, land_h,
-    load_sem, send_sem, recv_sem,
+    labels_hbm, owner_hbm, series_ref, out_ref,
+    labels_ref, owner_ref, raw, scored, panel, land_a, mid, land_b, whole,
+    part, land_e, half, land_h, load_sem, send_sem, recv_sem,
 ):
     grp, blk = lax.axis_index("grp"), lax.axis_index("blk")
     zi, yi = blk // NY, blk % NY
@@ -44,6 +45,12 @@
     other_core = {"grp": qi * NC + 1 - core}
 
     loads = []
+    small = [
+        pltpu.make_async_copy(owner_hbm, owner_ref, load_sem.at[3]),
+        pltpu.make_async_copy(labels_hbm, labels_ref, load_sem.at[4]),
+    ]
+    for copy in small:
+        copy.start()
     for k, (start, width) in enumerate(
         [(0, PANEL), (PANEL, PANEL), (STEPS * PANEL, COLUMNS - STEPS * PANEL)]
     ):
@@ -76,8 +83,6 @@
         )
         copy.start()
         return copy
-
-    started = []
 
     def standardize(s, start, step):
         cols = pl.ds(start, TILE)
@@ -99,9 +104,8 @@
             if step is not None:
                 mine = jnp.where(owner_ref[step] == blk, 1.0, 0.0)
                 turned = (y * mine).T.astype(jnp.bfloat16)
-                per = PANEL // CHUNK
-                panel[step, pl.ds(s * per, per), :, pl.ds(r, ROWS)] = turned.reshape(
-                    per, CHUNK, ROWS
+                panel[step, :, pl.ds(s * SHARE, SHARE), pl.ds(r, ROWS)] = turned.reshape(
+                    NZ, SHARE, ROWS
                 )
 
     rest = [
@@ -130,6 +134,7 @@
             src[...] += panel[k, d]
         a_copies[k, sign, t] = send(src, land_a.at[k, way, t], at_z(sign))
 
+    small[0].wait()
     for k in range(STEPS):
         loads[k].wait()
         for s in range(MEMBERS):
@@ -168,25 +173,7 @@
             )
     some_rest(8)
 
-    c_copies = {}
-
-    def send_c(k, sign, t):
-        if t:
-            c_copies[k, sign, t - 1].wait_recv()
-        d = (zi - sign * t + NZ) % NZ
-        c_copies[k, sign, t] = send(whole.at[k, d], whole.at[k, d], at_z(sign))
-
-    for k in range(STEPS):
-        for o in range(1, NY):
-            g_copies[k, o].wait_recv()
-        for sign in (1, -1):
-            send_c(k, sign, 0)
-    for t in range(1, 4):
-        for k in range(STEPS):
-            for sign in (1, -1):
-                if t < hops(k, sign):
-                    send_c(k, sign, t)
-
+    small[1].wait()
     halves = []
     for s in range(MEMBERS):
         label = labels_ref[grp * MEMBERS + s]
@@ -196,65 +183,114 @@
         counted = jnp.full((1, TILE), same.astype(jnp.float32))
         halves.append(0.5 / (COHORTS * counted))
 
-    d_copies = {}
-    for k in range(STEPS):
-        for sign in (1, -1):
-            c_copies[k, sign, hops(k, sign) - 1].wait_recv()
-
-        def tile(j, carry, k=k):
+    c_copies, e_copies = {}, {}
+
+    def send_c(k, sign, t):
+        d = (zi - sign * t + NZ) % NZ
+        c_copies[k, sign, t] = send(whole.at[k, d], whole.at[k, d], at_z(sign))
+
+    def compute(offsets):
+        chunks = [(zi + o + NZ) % NZ for o in offsets]
+
+        def tile(j, carry):
             cols = pl.ds(pl.multiple_of(j * TILE, TILE), TILE)
             total = None
-            per = NZ // MEMBERS
             for s in range(MEMBERS):
-                rows = whole[k, pl.ds(s * per, per)].reshape(PANEL, FRAMES)
+                rows = jnp.concatenate(
+                    [
+                        whole[k, d, pl.ds(s * NC, NC)].reshape(SHARE, FRAMES)
+                        for d in chunks
+                        for k in range(STEPS)
+                    ],
+                    axis=0,
+                )
                 q = jnp.dot(
                     rows, scored[s, :, cols], preferred_element_type=jnp.float32
                 ) * (1.0 / FRAMES)
                 q = jnp.clip(q, -clip_limit, clip_limit)
                 term = halves[s] * jnp.log((1.0 + q) / (1.0 - q))
                 total = term if total is None else total + term
-            part[k, :, :, :, cols] = total.astype(jnp.bfloat16).reshape(
-                NQ, NC, OUT_ROWS, TILE
+            total = total.astype(jnp.bfloat16).reshape(
+                len(chunks), STEPS, NC, OUT_ROWS, TILE
             )
+            for i, d in enumerate(chunks):
+                part[d, :, :, :, cols] = total[i]
             return carry
 
         lax.fori_loop(0, COLUMNS // TILE, tile, 0)
-        d_copies[k] = send(part.at[k, :, 1 - core], land_e.at[k], other_core)
-
-    h_copies = {}
-    for k in range(STEPS):
-        d_copies[k].wait_recv()
-        half[k] = (
-            part[k, :, core].astype(jnp.float32) + land_e[k].astype(jnp.float32)
-        ).astype(jnp.bfloat16)
-        for o in (4, 3, 5, 2, 6, 1, 7):
-            h_copies[k, o] = send(
-                half.at[k, (qi + o) % NQ], land_h.at[k, o - 1], at_q(o)
-            )
-    for k in range(STEPS):
-        total = half[k, qi].astype(jnp.float32)
-        for o in range(1, NQ):
-            h_copies[k, o].wait_recv()
-            total += land_h[k, o - 1].astype(jnp.float32)
-        out_ref[k] = total
-
-    for copies in (a_copies, b_copies, g_copies, c_copies, d_copies, h_copies):
+        for o, d in zip(offsets, chunks):
+            e_copies[o] = send(part.at[d, :, 1 - core], land_e.at[d], other_core)
+
+    base = count[0]
+    count[0] += NQ - 1
+
+    def h_copy(o, d):
+        k = base + o - 1
+        return pltpu.make_async_remote_copy(
+            src_ref=half.at[d],
+            dst_ref=land_h.at[o - 1],
+            send_sem=send_sem.at[k],
+            recv_sem=recv_sem.at[k],
+            device_id={"grp": d * NC + core},
+            device_id_type=MESH,
+        )
+
+    def forward(offsets):
+        for o in offsets:
+            d = (zi + o + NZ) % NZ
+            e_copies[o].wait_recv()
+            half[d] = (
+                part[d, :, core].astype(jnp.float32) + land_e[d].astype(jnp.float32)
+            ).astype(jnp.bfloat16)
+            away = (d - qi + NQ) % NQ
+
+            @pl.when(away != 0)
+            def _():
+                h_copy(away, d).start()
+
+    for k in range(STEPS):
+        for o in range(1, NY):
+            g_copies[k, o].wait_recv()
+        for sign in (1, -1):
+            send_c(k, sign, 0)
+    groups = [(0,), (1, -1), (2, -2), (3, -3), (4,)]
+    compute(groups[0])
+    for t in range(4):
+        for k in range(STEPS):
+            for sign in (1, -1):
+                if t < hops(k, sign):
+                    c_copies[k, sign, t].wait_recv()
+                if t + 1 < hops(k, sign):
+                    send_c(k, sign, t + 1)
+        forward(groups[t])
+        compute(groups[t + 1])
+    forward(groups[4])
+
+    total = half[qi].astype(jnp.float32)
+    for o in range(1, NQ):
+        h_copy(o, (qi + o) % NQ).wait_recv()
+        total += land_h[o - 1].astype(jnp.float32)
+    for k in range(STEPS):
+        upper = blk >= owner_ref[k]
+        out_ref[k] = jnp.where(upper, total[k], 0.0).astype(out_ref.dtype)
+
+    for copies in (a_copies, b_copies, g_copies, c_copies, e_copies):
         for copy in copies.values():
             copy.wait_send()
+    for o in range(1, NQ):
+        h_copy(o, (qi + o) % NQ).wait_send()
 
 
 def body(series, labels, panel_owner):
     half_type = jnp.bfloat16
-    summed = pl.pallas_call(
+    return pl.pallas_call(
         kernel,
-        out_shape=jax.ShapeDtypeStruct((STEPS, OUT_ROWS, COLUMNS), jnp.float32),
-        in_specs=[
-            pl.BlockSpec(memory_space=pltpu.SMEM),
-            pl.BlockSpec(memory_space=pltpu.SMEM),
-            pl.BlockSpec(memory_space=pl.ANY),
-        ],
+        out_shape=jax.ShapeDtypeStruct((STEPS, OUT_ROWS, COLUMNS), half_type),
+        in_specs=[pl.BlockSpec(memory_space=pltpu.HBM)] * 3,
         out_specs=pl.BlockSpec(memory_space=pltpu.VMEM),
         scratch_shapes=[
+            pltpu.SMEM((N_GRP * MEMBERS,), jnp.int32),
+            pltpu.SMEM((STEPS,), jnp.int32),
             pltpu.VMEM((MEMBERS, FRAMES, COLUMNS), half_type),
             pltpu.VMEM((MEMBERS, FRAMES, COLUMNS), half_type),
             pltpu.VMEM((STEPS, NZ, CHUNK, FRAMES), half_type),
@@ -262,20 +298,18 @@
             pltpu.VMEM((STEPS, NY, PIECE, FRAMES), half_type),
             pltpu.VMEM((STEPS, NY - 1, PIECE, FRAMES), half_type),
             pltpu.VMEM((STEPS, NZ, NY, PIECE, FRAMES), half_type),
-            pltpu.VMEM((STEPS, NQ, NC, OUT_ROWS, COLUMNS), half_type),
-            pltpu.VMEM((STEPS, NQ, OUT_ROWS, COLUMNS), half_type),
-            pltpu.VMEM((STEPS, NQ, OUT_ROWS, COLUMNS), half_type),
-            pltpu.VMEM((STEPS, NQ - 1, OUT_ROWS, COLUMNS), half_type),
-            pltpu.SemaphoreType.DMA((3,)),
+            pltpu.VMEM((NQ, STEPS, NC, OUT_ROWS, COLUMNS), half_type),
+            pltpu.VMEM((NQ, STEPS, OUT_ROWS, COLUMNS), half_type),
+            pltpu.VMEM((NQ, STEPS, OUT_ROWS, COLUMNS), half_type),
+            pltpu.VMEM((NQ - 1, STEPS, OUT_ROWS, COLUMNS), half_type),
+            pltpu.SemaphoreType.DMA((5,)),
             pltpu.SemaphoreType.DMA((N_COPIES,)),
             pltpu.SemaphoreType.DMA((N_COPIES,)),
         ],
         compiler_params=pltpu.CompilerParams(
-            collective_id=0, has_side_effects=True, vmem_limit_bytes=40 * 1024 * 1024
+            collective_id=0, has_side_effects=True, vmem_limit_bytes=60 * 1024 * 1024
         ),
     )(labels, panel_owner, series)
-    upper = lax.axis_index("blk") >= panel_owner
-    return jnp.where(upper[:, None, None], summed, 0.0).astype(jnp.bfloat16)
 
 
 def solution(mesh):

time: 75.6 us -> 70.6 us (0.934)
  the two profiles are of different devices: /device:TPU:1 before, /device:TPU:5 now
where the time goes in v2:
time: 70.6 us; the launch traced here: 70.4 us
  Pallas kernels  68.9 us (98%)
  local copies, waits for them, and re-layouts  1.54 us (2%)
    pallas_call x1, Pallas kernels, body(): pl.pallas_call(kernel, out_shape=jax.ShapeDtypeStruct((STEPS, OUT_ROWS, C...  68.9 us
    unnamed x1, local copies, waits for them, and re-layouts  1.54 us

profile of v2, /device:TPU:5, one launch (start us, length us, event | category | flops | bytes accessed | tf_op | source)
XLA Modules:
  0.0 70.4 jit_solution(11333388684410195940)
XLA Ops:
  0.0 68.9 %shard_map.37 = bf16[2,16,1536]{2,1,0:T(8,128)(2,1)} custom-call(s32[32]{0:T(128)} %labels_hbm.1, s32[2]{0:T(128)} %owner_hbm.1, bf16[2,512,1536]{2,1,0:T(8,128)(2,1)} %series_ref.1), custom_call_target="tpu_custom_call" | custom-call | tf_op jit(solution)/shard_map/pallas_call | solution.py:286
  68.9 1.5 %copy.5 = bf16[2,16,1536]{2,1,0:T(8,128)(2,1)} copy(bf16[2,16,1536]{2,1,0:T(8,128)(2,1)} %shard_map.37) | data formatting | bytes 196608

commit v3 on v2

--- a/solution.py
+++ b/solution.py
@@ -21,7 +21,7 @@
 epsilon = 1e-05
 clip_limit = 0.99
 
-N_COPIES = STEPS * (7 + 6 + 7) + NQ + NQ - 1
+N_COPIES = STEPS * (7 + 7) + 6 + NQ + NQ - 1
 
 
 def kernel(
@@ -61,7 +61,7 @@
         loads[-1].start()
 
     barrier = pltpu.get_barrier_semaphore()
-    peers = [at_z(1), at_z(-1)]
+    peers = [at_z(o) for o in (1, -1, 2, -2)]
     peers += [at_y(o) for o in range(1, NY)]
     peers += [other_core]
     peers += [at_q(o) for o in range(1, NQ)]
@@ -117,21 +117,28 @@
             if rest:
                 standardize(*rest.pop(0), None)
 
-    def hops(k, sign):
-        return 4 if (sign > 0) == (k == 0) else 3
+    def far(k, sign):
+        return (sign > 0) == (k == 0)
 
     a_copies = {}
 
     def send_a(k, sign, t):
-        reach = hops(k, sign)
-        d = (zi + sign * (reach - t) + NZ) % NZ
         way = 0 if sign > 0 else 1
+        d = (zi + sign * (3 - t) + NZ) % NZ
         if t == 0:
+            if far(k, sign):
+                a_copies[k, sign, 3] = send(
+                    panel.at[k, (zi + 4) % NZ], land_a.at[k, way, 3], at_z(2 * sign)
+                )
             src = panel.at[k, d]
         else:
             a_copies[k, sign, t - 1].wait_recv()
             src = land_a.at[k, way, t - 1]
-            src[...] += panel[k, d]
+            if t == 1 and far(k, sign):
+                a_copies[k, sign, 3].wait_recv()
+                src[...] += panel[k, d] + land_a[k, way, 3]
+            else:
+                src[...] += panel[k, d]
         a_copies[k, sign, t] = send(src, land_a.at[k, way, t], at_z(sign))
 
     small[0].wait()
@@ -144,34 +151,28 @@
         for sign in (1, -1):
             send_a(k, sign, 0)
     loads[2].wait()
-    for t in range(1, 4):
-        some_rest(2)
+    for t in range(1, 3):
+        some_rest(3)
         for k in range(STEPS):
             for sign in (1, -1):
-                if t < hops(k, sign):
-                    send_a(k, sign, t)
+                send_a(k, sign, t)
     some_rest(2)
 
-    b_copies = {}
     for k in range(STEPS):
         for sign in (1, -1):
-            a_copies[k, sign, hops(k, sign) - 1].wait_recv()
-        got = [land_a[k, w, hops(k, sign) - 1] for w, sign in ((0, 1), (1, -1))]
-        mid[k] = (panel[k, zi] + got[0] + got[1]).reshape(NY, PIECE, FRAMES)
-        for o in (2, 1, 3):
-            b_copies[k, o] = send(
-                mid.at[k, (yi + o) % NY], land_b.at[k, o - 1], at_y(o)
-            )
+            a_copies[k, sign, 2].wait_recv()
+        mid[:, k] = (panel[k, zi] + land_a[k, 0, 2] + land_a[k, 1, 2]).reshape(
+            NY, PIECE, FRAMES
+        )
+    b_copies = {}
+    for o in (2, 1, 3):
+        b_copies[o] = send(mid.at[(yi + o) % NY], land_b.at[o - 1], at_y(o))
+    for o in range(1, NY):
+        b_copies[o].wait_recv()
+    whole[zi, yi] = mid[yi] + land_b[0] + land_b[1] + land_b[2]
     g_copies = {}
-    for k in range(STEPS):
-        for o in range(1, NY):
-            b_copies[k, o].wait_recv()
-        whole[k, zi, yi] = mid[k, yi] + land_b[k, 0] + land_b[k, 1] + land_b[k, 2]
-        for o in (2, 1, 3):
-            g_copies[k, o] = send(
-                whole.at[k, zi, yi], whole.at[k, zi, yi], at_y(o)
-            )
-    some_rest(8)
+    for o in (2, 1, 3):
+        g_copies[o] = send(whole.at[zi, yi], whole.at[zi, yi], at_y(o))
 
     small[1].wait()
     halves = []
@@ -187,7 +188,10 @@
 
     def send_c(k, sign, t):
         d = (zi - sign * t + NZ) % NZ
-        c_copies[k, sign, t] = send(whole.at[k, d], whole.at[k, d], at_z(sign))
+        chunk = whole.at[d, :, k]
+        if t == 2 and far(k, sign):
+            c_copies[k, sign, 3] = send(chunk, chunk, at_z(2 * sign))
+        c_copies[k, sign, t] = send(chunk, chunk, at_z(sign))
 
     def compute(offsets):
         chunks = [(zi + o + NZ) % NZ for o in offsets]
@@ -198,9 +202,8 @@
             for s in range(MEMBERS):
                 rows = jnp.concatenate(
                     [
-                        whole[k, d, pl.ds(s * NC, NC)].reshape(SHARE, FRAMES)
+                        whole[d, pl.ds(s * NC, NC)].reshape(STEPS * SHARE, FRAMES)
                         for d in chunks
-                        for k in range(STEPS)
                     ],
                     axis=0,
                 )
@@ -211,7 +214,7 @@
                 term = halves[s] * jnp.log((1.0 + q) / (1.0 - q))
                 total = term if total is None else total + term
             total = total.astype(jnp.bfloat16).reshape(
-                len(chunks), STEPS, NC, OUT_ROWS, TILE
+                len(chunks), NC, STEPS, OUT_ROWS, TILE
             )
             for i, d in enumerate(chunks):
                 part[d, :, :, :, cols] = total[i]
@@ -219,7 +222,7 @@
 
         lax.fori_loop(0, COLUMNS // TILE, tile, 0)
         for o, d in zip(offsets, chunks):
-            e_copies[o] = send(part.at[d, :, 1 - core], land_e.at[d], other_core)
+            e_copies[o] = send(part.at[d, 1 - core], land_e.at[d], other_core)
 
     base = count[0]
     count[0] += NQ - 1
@@ -240,7 +243,7 @@
             d = (zi + o + NZ) % NZ
             e_copies[o].wait_recv()
             half[d] = (
-                part[d, :, core].astype(jnp.float32) + land_e[d].astype(jnp.float32)
+                part[d, core].astype(jnp.float32) + land_e[d].astype(jnp.float32)
             ).astype(jnp.bfloat16)
             away = (d - qi + NQ) % NQ
 
@@ -248,23 +251,28 @@
             def _():
                 h_copy(away, d).start()
 
+    for o in range(1, NY):
+        g_copies[o].wait_recv()
     for k in range(STEPS):
-        for o in range(1, NY):
-            g_copies[k, o].wait_recv()
         for sign in (1, -1):
             send_c(k, sign, 0)
-    groups = [(0,), (1, -1), (2, -2), (3, -3), (4,)]
-    compute(groups[0])
-    for t in range(4):
+    compute((0,))
+    for t in range(1, 3):
         for k in range(STEPS):
             for sign in (1, -1):
-                if t < hops(k, sign):
+                c_copies[k, sign, t - 1].wait_recv()
+                send_c(k, sign, t)
+        forward((0,) if t == 1 else (1, -1))
+        compute((t, -t))
+    for t in (3, 2):
+        for k in range(STEPS):
+            for sign in (1, -1):
+                if (k, sign, t) in c_copies:
                     c_copies[k, sign, t].wait_recv()
-                if t + 1 < hops(k, sign):
-                    send_c(k, sign, t + 1)
-        forward(groups[t])
-        compute(groups[t + 1])
-    forward(groups[4])
+    forward((2, -2))
+    compute((3, -3))
+    compute((4,))
+    forward((3, -3, 4))
 
     total = half[qi].astype(jnp.float32)
     for o in range(1, NQ):
@@ -272,7 +280,7 @@
         total += land_h[o - 1].astype(jnp.float32)
     for k in range(STEPS):
         upper = blk >= owner_ref[k]
-        out_ref[k] = jnp.where(upper, total[k], 0.0).astype(out_ref.dtype)
+        out_ref[k] = jnp.where(upper, total[k], 0.0)
 
     for copies in (a_copies, b_copies, g_copies, c_copies, e_copies):
         for copy in copies.values():
@@ -283,9 +291,9 @@
 
 def body(series, labels, panel_owner):
     half_type = jnp.bfloat16
-    return pl.pallas_call(
+    summed = pl.pallas_call(
         kernel,
-        out_shape=jax.ShapeDtypeStruct((STEPS, OUT_ROWS, COLUMNS), half_type),
+        out_shape=jax.ShapeDtypeStruct((STEPS, OUT_ROWS, COLUMNS), jnp.float32),
         in_specs=[pl.BlockSpec(memory_space=pltpu.HBM)] * 3,
         out_specs=pl.BlockSpec(memory_space=pltpu.VMEM),
         scratch_shapes=[
@@ -295,10 +303,10 @@
             pltpu.VMEM((MEMBERS, FRAMES, COLUMNS), half_type),
             pltpu.VMEM((STEPS, NZ, CHUNK, FRAMES), half_type),
             pltpu.VMEM((STEPS, 2, 4, CHUNK, FRAMES), half_type),
-            pltpu.VMEM((STEPS, NY, PIECE, FRAMES), half_type),
-            pltpu.VMEM((STEPS, NY - 1, PIECE, FRAMES), half_type),
-            pltpu.VMEM((STEPS, NZ, NY, PIECE, FRAMES), half_type),
-            pltpu.VMEM((NQ, STEPS, NC, OUT_ROWS, COLUMNS), half_type),
+            pltpu.VMEM((NY, STEPS, PIECE, FRAMES), half_type),
+            pltpu.VMEM((NY - 1, STEPS, PIECE, FRAMES), half_type),
+            pltpu.VMEM((NZ, NY, STEPS, PIECE, FRAMES), half_type),
+            pltpu.VMEM((NQ, NC, STEPS, OUT_ROWS, COLUMNS), half_type),
             pltpu.VMEM((NQ, STEPS, OUT_ROWS, COLUMNS), half_type),
             pltpu.VMEM((NQ, STEPS, OUT_ROWS, COLUMNS), half_type),
             pltpu.VMEM((NQ - 1, STEPS, OUT_ROWS, COLUMNS), half_type),
@@ -310,6 +318,7 @@
             collective_id=0, has_side_effects=True, vmem_limit_bytes=60 * 1024 * 1024
         ),
     )(labels, panel_owner, series)
+    return summed.astype(half_type)
 
 
 def solution(mesh):

time: 70.6 us -> 72.1 us (1.021)
  other arithmetic: 0 us -> 1.58 us
  local copies, waits for them, and re-layouts: 1.54 us -> 0 us
  Pallas kernels: 68.9 us -> 70.4 us
    convert_element_type x0 -> x1, other arithmetic: none -> 1.58 us  [body(): return summed.astype(half_type)]
    unnamed x1 -> x0, local copies, waits for them, and re-layouts: 1.54 us -> none
    pallas_call x1, Pallas kernels: 68.9 us -> 70.4 us  [body(): pl.pallas_call(kernel, out_shape=jax.ShapeDtypeStruct((STEPS, OUT_ROWS, C...]
where the time goes in v3:
time: 72.1 us; the launch traced here: 72 us
  Pallas kernels  70.4 us (98%)
  other arithmetic  1.58 us (2%)
    pallas_call x1, Pallas kernels, body(): pl.pallas_call(kernel, out_shape=jax.ShapeDtypeStruct((STEPS, OUT_ROWS, C...  70.4 us
    convert_element_type x1, other arithmetic, body(): return summed.astype(half_type)  1.58 us

profile of v3, /device:TPU:5, one launch (start us, length us, event | category | flops | bytes accessed | tf_op | source)
XLA Modules:
  0.0 72.0 jit_solution(6415472109094091638)
XLA Ops:
  0.0 70.4 %shard_map.37 = f32[2,16,1536]{2,1,0:T(8,128)} custom-call(s32[32]{0:T(128)} %labels_hbm.1, s32[2]{0:T(128)} %owner_hbm.1, bf16[2,512,1536]{2,1,0:T(8,128)(2,1)} %series_ref.1), custom_call_target="tpu_custom_call" | custom-call | tf_op jit(solution)/shard_map/pallas_call | solution.py:294
  70.4 1.6 %convert_element_type.3 = bf16[2,16,1536]{2,1,0:T(8,128)(2,1)} convert(f32[2,16,1536]{2,1,0:T(8,128)} %shard_map.37) | non-fusion elementwise | flops 49152 | bytes 294912 | tf_op jit(solution)/shard_map/convert_element_type | solution.py:321

commit v4 on v3

--- a/solution.py
+++ b/solution.py
@@ -12,16 +12,15 @@
 FRAMES, COLUMNS = 512, 1536
 NZ, NY, NQ, NC = 8, 4, 8, 2
 N_GRP, N_BLK = NQ * NC, NZ * NY
-CHUNK = MEMBERS * PANEL // NZ
-PIECE = CHUNK // NY
-SHARE = PANEL // NZ
+PIECE = PANEL // NZ
 OUT_ROWS = PANEL // N_GRP
 TILE = 256
+WIDE = 512
 ROWS = 128
 epsilon = 1e-05
 clip_limit = 0.99
 
-N_COPIES = STEPS * (7 + 7) + 6 + NQ + NQ - 1
+N_COPIES = NY * (7 + 7) + 6 + NQ + NQ - 1
 
 
 def kernel(
@@ -61,10 +60,10 @@
         loads[-1].start()
 
     barrier = pltpu.get_barrier_semaphore()
-    peers = [at_z(o) for o in (1, -1, 2, -2)]
-    peers += [at_y(o) for o in range(1, NY)]
+    peers = [at_y(o) for o in (2, 1, 3)]
+    peers += [at_z(o) for o in (1, -1, 2, -2)]
+    peers += [at_q(o) for o in range(1, NQ)]
     peers += [other_core]
-    peers += [at_q(o) for o in range(1, NQ)]
     for peer in peers:
         pl.semaphore_signal(barrier, inc=1, device_id=peer, device_id_type=MESH)
 
@@ -104,8 +103,8 @@
             if step is not None:
                 mine = jnp.where(owner_ref[step] == blk, 1.0, 0.0)
                 turned = (y * mine).T.astype(jnp.bfloat16)
-                panel[step, :, pl.ds(s * SHARE, SHARE), pl.ds(r, ROWS)] = turned.reshape(
-                    NZ, SHARE, ROWS
+                panel[:, s * STEPS + step, :, pl.ds(r, ROWS)] = turned.reshape(
+                    NZ, PIECE, ROWS
                 )
 
     rest = [
@@ -117,62 +116,74 @@
             if rest:
                 standardize(*rest.pop(0), None)
 
-    def far(k, sign):
-        return (sign > 0) == (k == 0)
-
+    def far(o, sign):
+        return (sign > 0) == (o % 2 == 0)
+
+    SIGNS = (1, -1)
     a_copies = {}
 
-    def send_a(k, sign, t):
+    def send_a(o, sign, t):
         way = 0 if sign > 0 else 1
-        d = (zi + sign * (3 - t) + NZ) % NZ
+        j = (yi + o) % NY
+        mine = panel.at[(zi + sign * (3 - t) + NZ) % NZ, j]
         if t == 0:
-            if far(k, sign):
-                a_copies[k, sign, 3] = send(
-                    panel.at[k, (zi + 4) % NZ], land_a.at[k, way, 3], at_z(2 * sign)
+            if far(o, sign):
+                a_copies[o, sign, 3] = send(
+                    panel.at[(zi + 4) % NZ, j], land_a.at[o, way, 3], at_z(2 * sign)
                 )
-            src = panel.at[k, d]
+            src = mine
         else:
-            a_copies[k, sign, t - 1].wait_recv()
-            src = land_a.at[k, way, t - 1]
-            if t == 1 and far(k, sign):
-                a_copies[k, sign, 3].wait_recv()
-                src[...] += panel[k, d] + land_a[k, way, 3]
+            a_copies[o, sign, t - 1].wait_recv()
+            src = land_a.at[o, way, t - 1]
+            if t == 1 and far(o, sign):
+                a_copies[o, sign, 3].wait_recv()
+                src[...] += mine[...] + land_a[o, way, 3]
             else:
-                src[...] += panel[k, d]
-        a_copies[k, sign, t] = send(src, land_a.at[k, way, t], at_z(sign))
+                src[...] += mine[...]
+        a_copies[o, sign, t] = send(src, land_a.at[o, way, t], at_z(sign))
 
     small[0].wait()
     for k in range(STEPS):
         loads[k].wait()
         for s in range(MEMBERS):
             standardize(s, k * PANEL, k)
-        if k == 0:
-            pl.semaphore_wait(barrier, len(peers))
-        for sign in (1, -1):
-            send_a(k, sign, 0)
+    pl.semaphore_wait(barrier, len(peers))
+    order = (2, 1, 3, 0)
+    for o in order:
+        for sign in SIGNS:
+            send_a(o, sign, 0)
     loads[2].wait()
+    some_rest(4)
     for t in range(1, 3):
-        some_rest(3)
-        for k in range(STEPS):
-            for sign in (1, -1):
-                send_a(k, sign, t)
-    some_rest(2)
-
-    for k in range(STEPS):
-        for sign in (1, -1):
-            a_copies[k, sign, 2].wait_recv()
-        mid[:, k] = (panel[k, zi] + land_a[k, 0, 2] + land_a[k, 1, 2]).reshape(
-            NY, PIECE, FRAMES
-        )
+        for o in order:
+            for sign in SIGNS:
+                send_a(o, sign, t)
+        some_rest(2)
+
     b_copies = {}
-    for o in (2, 1, 3):
-        b_copies[o] = send(mid.at[(yi + o) % NY], land_b.at[o - 1], at_y(o))
-    for o in range(1, NY):
+    for o in order:
+        for sign in SIGNS:
+            a_copies[o, sign, 2].wait_recv()
+        mid[o] = panel[zi, (yi + o) % NY] + land_a[o, 0, 2] + land_a[o, 1, 2]
+        if o:
+            b_copies[o] = send(mid.at[o], land_b.at[o - 1], at_y(o))
+    for o in (1, 3, 2):
         b_copies[o].wait_recv()
-    whole[zi, yi] = mid[yi] + land_b[0] + land_b[1] + land_b[2]
-    g_copies = {}
+    whole[zi, yi] = mid[0] + land_b[0] + land_b[1] + land_b[2]
+    g_copies, c_copies = {}, {}
+
+    def send_c(o, sign, t):
+        if t:
+            c_copies[o, sign, t - 1].wait_recv()
+        piece = whole.at[(zi - sign * t + NZ) % NZ, (yi - o + NY) % NY]
+        if t == 2 and far(o, sign):
+            c_copies[o, sign, 3] = send(piece, piece, at_z(2 * sign))
+        c_copies[o, sign, t] = send(piece, piece, at_z(sign))
+
     for o in (2, 1, 3):
         g_copies[o] = send(whole.at[zi, yi], whole.at[zi, yi], at_y(o))
+    for sign in SIGNS:
+        send_c(0, sign, 0)
 
     small[1].wait()
     halves = []
@@ -181,28 +192,21 @@
         same = jnp.int32(0)
         for i in range(N_GRP * MEMBERS):
             same += jnp.where(labels_ref[i] == label, 1, 0)
-        counted = jnp.full((1, TILE), same.astype(jnp.float32))
+        counted = jnp.full((1, WIDE), same.astype(jnp.float32))
         halves.append(0.5 / (COHORTS * counted))
 
-    c_copies, e_copies = {}, {}
-
-    def send_c(k, sign, t):
-        d = (zi - sign * t + NZ) % NZ
-        chunk = whole.at[d, :, k]
-        if t == 2 and far(k, sign):
-            c_copies[k, sign, 3] = send(chunk, chunk, at_z(2 * sign))
-        c_copies[k, sign, t] = send(chunk, chunk, at_z(sign))
+    e_copies = {}
 
     def compute(offsets):
         chunks = [(zi + o + NZ) % NZ for o in offsets]
 
         def tile(j, carry):
-            cols = pl.ds(pl.multiple_of(j * TILE, TILE), TILE)
+            cols = pl.ds(pl.multiple_of(j * WIDE, WIDE), WIDE)
             total = None
             for s in range(MEMBERS):
                 rows = jnp.concatenate(
                     [
-                        whole[d, pl.ds(s * NC, NC)].reshape(STEPS * SHARE, FRAMES)
+                        whole[d, pl.ds(s * STEPS, STEPS)].reshape(STEPS * PIECE, FRAMES)
                         for d in chunks
                     ],
                     axis=0,
@@ -211,16 +215,18 @@
                     rows, scored[s, :, cols], preferred_element_type=jnp.float32
                 ) * (1.0 / FRAMES)
                 q = jnp.clip(q, -clip_limit, clip_limit)
-                term = halves[s] * jnp.log((1.0 + q) / (1.0 - q))
+                term = halves[s] * (jnp.log(1.0 + q) - jnp.log(1.0 - q))
                 total = term if total is None else total + term
             total = total.astype(jnp.bfloat16).reshape(
-                len(chunks), NC, STEPS, OUT_ROWS, TILE
+                len(chunks), STEPS, NC, OUT_ROWS, WIDE
             )
             for i, d in enumerate(chunks):
-                part[d, :, :, :, cols] = total[i]
+                for k in range(STEPS):
+                    for c in range(NC):
+                        part[d, c, k, :, cols] = total[i, k, c]
             return carry
 
-        lax.fori_loop(0, COLUMNS // TILE, tile, 0)
+        lax.fori_loop(0, COLUMNS // WIDE, tile, 0)
         for o, d in zip(offsets, chunks):
             e_copies[o] = send(part.at[d, 1 - core], land_e.at[d], other_core)
 
@@ -251,26 +257,37 @@
             def _():
                 h_copy(away, d).start()
 
-    for o in range(1, NY):
-        g_copies[o].wait_recv()
-    for k in range(STEPS):
-        for sign in (1, -1):
-            send_c(k, sign, 0)
+    def hop(o, t):
+        if t == 0:
+            g_copies[o].wait_recv()
+        for sign in SIGNS:
+            send_c(o, sign, t)
+
+    hop(1, 0)
+    hop(3, 0)
+    hop(0, 1)
+    hop(2, 0)
     compute((0,))
-    for t in range(1, 3):
-        for k in range(STEPS):
-            for sign in (1, -1):
-                c_copies[k, sign, t - 1].wait_recv()
-                send_c(k, sign, t)
-        forward((0,) if t == 1 else (1, -1))
-        compute((t, -t))
-    for t in (3, 2):
-        for k in range(STEPS):
-            for sign in (1, -1):
-                if (k, sign, t) in c_copies:
-                    c_copies[k, sign, t].wait_recv()
+    hop(1, 1)
+    hop(3, 1)
+    hop(0, 2)
+    hop(2, 1)
+    forward((0,))
+    compute((1, -1))
+    hop(1, 2)
+    hop(3, 2)
+    hop(2, 2)
+    forward((1, -1))
+    compute((2, -2))
     forward((2, -2))
+    for o in (0, 1, 3, 2):
+        for sign in SIGNS:
+            c_copies[o, sign, 2].wait_recv()
     compute((3, -3))
+    for o in (0, 1, 3, 2):
+        for sign in SIGNS:
+            if far(o, sign):
+                c_copies[o, sign, 3].wait_recv()
     compute((4,))
     forward((3, -3, 4))
 
@@ -301,11 +318,11 @@
             pltpu.SMEM((STEPS,), jnp.int32),
             pltpu.VMEM((MEMBERS, FRAMES, COLUMNS), half_type),
             pltpu.VMEM((MEMBERS, FRAMES, COLUMNS), half_type),
-            pltpu.VMEM((STEPS, NZ, CHUNK, FRAMES), half_type),
-            pltpu.VMEM((STEPS, 2, 4, CHUNK, FRAMES), half_type),
-            pltpu.VMEM((NY, STEPS, PIECE, FRAMES), half_type),
-            pltpu.VMEM((NY - 1, STEPS, PIECE, FRAMES), half_type),
-            pltpu.VMEM((NZ, NY, STEPS, PIECE, FRAMES), half_type),
+            pltpu.VMEM((NZ, NY, PIECE, FRAMES), half_type),
+            pltpu.VMEM((NY, 2, 4, PIECE, FRAMES), half_type),
+            pltpu.VMEM((NY, PIECE, FRAMES), half_type),
+            pltpu.VMEM((NY - 1, PIECE, FRAMES), half_type),
+            pltpu.VMEM((NZ, NY, PIECE, FRAMES), half_type),
             pltpu.VMEM((NQ, NC, STEPS, OUT_ROWS, COLUMNS), half_type),
             pltpu.VMEM((NQ, STEPS, OUT_ROWS, COLUMNS), half_type),
             pltpu.VMEM((NQ, STEPS, OUT_ROWS, COLUMNS), half_type),

time: 72.1 us -> 67.1 us (0.931)
  the two profiles are of different devices: /device:TPU:5 before, /device:TPU:12 now
where the time goes in v4:
time: 67.1 us; the launch traced here: 66.9 us
  Pallas kernels  65.3 us (97%)
  other arithmetic  1.58 us (2%)
    pallas_call x1, Pallas kernels, body(): pl.pallas_call(kernel, out_shape=jax.ShapeDtypeStruct((STEPS, OUT_ROWS, C...  65.3 us
    convert_element_type x1, other arithmetic, body(): return summed.astype(half_type)  1.58 us

profile of v4, /device:TPU:12, one launch (start us, length us, event | category | flops | bytes accessed | tf_op | source)
XLA Modules:
  0.0 66.9 jit_solution(11548300038630262471)
XLA Ops:
  0.0 65.3 %shard_map.37 = f32[2,16,1536]{2,1,0:T(8,128)} custom-call(s32[32]{0:T(128)} %labels_hbm.1, s32[2]{0:T(128)} %owner_hbm.1, bf16[2,512,1536]{2,1,0:T(8,128)(2,1)} %series_ref.1), custom_call_target="tpu_custom_call" | custom-call | tf_op jit(solution)/shard_map/pallas_call | solution.py:311
  65.3 1.6 %convert_element_type.3 = bf16[2,16,1536]{2,1,0:T(8,128)(2,1)} convert(f32[2,16,1536]{2,1,0:T(8,128)} %shard_map.37) | non-fusion elementwise | flops 49152 | bytes 294912 | tf_op jit(solution)/shard_map/convert_element_type | solution.py:338

commit v5 on v4

--- a/solution.py
+++ b/solution.py
@@ -20,7 +20,7 @@
 epsilon = 1e-05
 clip_limit = 0.99
 
-N_COPIES = NY * (7 + 7) + 6 + NQ + NQ - 1
+N_COPIES = NY * (7 + 7) + 6 + NQ + 3 + STEPS * (NQ - 1)
 
 
 def kernel(
@@ -45,19 +45,28 @@
 
     loads = []
     small = [
-        pltpu.make_async_copy(owner_hbm, owner_ref, load_sem.at[3]),
-        pltpu.make_async_copy(labels_hbm, labels_ref, load_sem.at[4]),
+        pltpu.make_async_copy(owner_hbm, owner_ref, load_sem.at[NY + 1]),
+        pltpu.make_async_copy(labels_hbm, labels_ref, load_sem.at[NY + 2]),
     ]
     for copy in small:
         copy.start()
-    for k, (start, width) in enumerate(
-        [(0, PANEL), (PANEL, PANEL), (STEPS * PANEL, COLUMNS - STEPS * PANEL)]
-    ):
-        window = (slice(None), slice(None), pl.ds(start, width))
+    order = (2, 1, 3, 0)
+    for i, o in enumerate(order):
+        s, k = (yi + o) % NY // STEPS, (yi + o) % STEPS
+        cols = pl.ds(pl.multiple_of(k * PANEL, PANEL), PANEL)
         loads.append(
-            pltpu.make_async_copy(series_ref.at[window], raw.at[window], load_sem.at[k])
+            pltpu.make_async_copy(
+                series_ref.at[s, :, cols], raw.at[s, :, cols], load_sem.at[i]
+            )
         )
         loads[-1].start()
+    cols = pl.ds(STEPS * PANEL, COLUMNS - STEPS * PANEL)
+    loads.append(
+        pltpu.make_async_copy(
+            series_ref.at[:, :, cols], raw.at[:, :, cols], load_sem.at[NY]
+        )
+    )
+    loads[-1].start()
 
     barrier = pltpu.get_barrier_semaphore()
     peers = [at_y(o) for o in (2, 1, 3)]
@@ -84,7 +93,7 @@
         return copy
 
     def standardize(s, start, step):
-        cols = pl.ds(start, TILE)
+        cols = pl.ds(pl.multiple_of(start, TILE), TILE)
         total = jnp.zeros((8, TILE), jnp.float32)
         for r in range(0, FRAMES, ROWS):
             x = raw[s, pl.ds(r, ROWS), cols].astype(jnp.float32)
@@ -103,9 +112,12 @@
             if step is not None:
                 mine = jnp.where(owner_ref[step] == blk, 1.0, 0.0)
                 turned = (y * mine).T.astype(jnp.bfloat16)
-                panel[:, s * STEPS + step, :, pl.ds(r, ROWS)] = turned.reshape(
-                    NZ, PIECE, ROWS
-                )
+                turned = turned.reshape(2, NZ // 2, PIECE, ROWS)
+                for i in range(2):
+                    at = NZ // 2 * (i + step - 2 * i * step)
+                    panel[
+                        pl.ds(at, NZ // 2), s * STEPS + step, :, pl.ds(r, ROWS)
+                    ] = turned[i]
 
     rest = [
         (s, c) for s in range(MEMBERS) for c in range(STEPS * PANEL, COLUMNS, TILE)
@@ -143,16 +155,15 @@
         a_copies[o, sign, t] = send(src, land_a.at[o, way, t], at_z(sign))
 
     small[0].wait()
-    for k in range(STEPS):
-        loads[k].wait()
-        for s in range(MEMBERS):
-            standardize(s, k * PANEL, k)
-    pl.semaphore_wait(barrier, len(peers))
-    order = (2, 1, 3, 0)
-    for o in order:
+    for i, o in enumerate(order):
+        loads[i].wait()
+        s, k = (yi + o) % NY // STEPS, (yi + o) % STEPS
+        standardize(s, k * PANEL, k)
+        if i == 0:
+            pl.semaphore_wait(barrier, len(peers))
         for sign in SIGNS:
             send_a(o, sign, 0)
-    loads[2].wait()
+    loads[NY].wait()
     some_rest(4)
     for t in range(1, 3):
         for o in order:
@@ -195,10 +206,9 @@
         counted = jnp.full((1, WIDE), same.astype(jnp.float32))
         halves.append(0.5 / (COHORTS * counted))
 
-    e_copies = {}
-
-    def compute(offsets):
+    def compute(offsets, step=None):
         chunks = [(zi + o + NZ) % NZ for o in offsets]
+        first, steps = (0, STEPS) if step is None else (step, 1)
 
         def tile(j, carry):
             cols = pl.ds(pl.multiple_of(j * WIDE, WIDE), WIDE)
@@ -206,7 +216,9 @@
             for s in range(MEMBERS):
                 rows = jnp.concatenate(
                     [
-                        whole[d, pl.ds(s * STEPS, STEPS)].reshape(STEPS * PIECE, FRAMES)
+                        whole[d, pl.ds(s * STEPS + first, steps)].reshape(
+                            steps * PIECE, FRAMES
+                        )
                         for d in chunks
                     ],
                     axis=0,
@@ -218,44 +230,49 @@
                 term = halves[s] * (jnp.log(1.0 + q) - jnp.log(1.0 - q))
                 total = term if total is None else total + term
             total = total.astype(jnp.bfloat16).reshape(
-                len(chunks), STEPS, NC, OUT_ROWS, WIDE
+                len(chunks), steps, NC, OUT_ROWS, WIDE
             )
             for i, d in enumerate(chunks):
-                for k in range(STEPS):
+                for k in range(steps):
                     for c in range(NC):
-                        part[d, c, k, :, cols] = total[i, k, c]
+                        part[d, c, first + k, :, cols] = total[i, k, c]
             return carry
 
         lax.fori_loop(0, COLUMNS // WIDE, tile, 0)
-        for o, d in zip(offsets, chunks):
-            e_copies[o] = send(part.at[d, 1 - core], land_e.at[d], other_core)
+        mine = pl.ds(first, steps)
+        return [
+            send(part.at[d, 1 - core, mine], land_e.at[d, mine], other_core)
+            for d in chunks
+        ]
 
     base = count[0]
-    count[0] += NQ - 1
-
-    def h_copy(o, d):
-        k = base + o - 1
+    count[0] += STEPS * (NQ - 1)
+
+    def h_copy(away, d, k):
+        at = base + (away - 1) * STEPS + k
         return pltpu.make_async_remote_copy(
-            src_ref=half.at[d],
-            dst_ref=land_h.at[o - 1],
-            send_sem=send_sem.at[k],
-            recv_sem=recv_sem.at[k],
-            device_id={"grp": d * NC + core},
+            src_ref=half.at[d, k],
+            dst_ref=land_h.at[away - 1, k],
+            send_sem=send_sem.at[at],
+            recv_sem=recv_sem.at[at],
+            device_id=at_q(away),
             device_id_type=MESH,
         )
 
-    def forward(offsets):
-        for o in offsets:
+    def forward(offsets, copies, steps=range(STEPS)):
+        for o, copy in zip(offsets, copies):
             d = (zi + o + NZ) % NZ
-            e_copies[o].wait_recv()
-            half[d] = (
-                part[d, core].astype(jnp.float32) + land_e[d].astype(jnp.float32)
-            ).astype(jnp.bfloat16)
-            away = (d - qi + NQ) % NQ
-
-            @pl.when(away != 0)
-            def _():
-                h_copy(away, d).start()
+            copy.wait_recv()
+            for k in steps:
+                half[d, k] = (
+                    part[d, core, k].astype(jnp.float32)
+                    + land_e[d, k].astype(jnp.float32)
+                ).astype(jnp.bfloat16)
+                away = (d + NQ // 2 * k - qi + NQ) % NQ
+
+                @pl.when(away != 0)
+                def _():
+                    h_copy(away, d, k).start()
 
     def hop(o, t):
         if t == 0:
@@ -267,43 +284,47 @@
     hop(3, 0)
     hop(0, 1)
     hop(2, 0)
-    compute((0,))
+    near = compute((0,))
     hop(1, 1)
     hop(3, 1)
     hop(0, 2)
     hop(2, 1)
-    forward((0,))
-    compute((1, -1))
+    forward((0,), near)
+    next_one = compute((1, -1))
     hop(1, 2)
     hop(3, 2)
     hop(2, 2)
-    forward((1, -1))
-    compute((2, -2))
-    forward((2, -2))
-    for o in (0, 1, 3, 2):
-        for sign in SIGNS:
-            c_copies[o, sign, 2].wait_recv()
-    compute((3, -3))
-    for o in (0, 1, 3, 2):
-        for sign in SIGNS:
-            if far(o, sign):
-                c_copies[o, sign, 3].wait_recv()
-    compute((4,))
-    forward((3, -3, 4))
-
-    total = half[qi].astype(jnp.float32)
-    for o in range(1, NQ):
-        h_copy(o, (qi + o) % NQ).wait_recv()
-        total += land_h[o - 1].astype(jnp.float32)
+    forward((1, -1), next_one)
+    next_two = compute((2, -2))
+    forward((2, -2), next_two)
+    last = []
+    for pair in ((1, 3), (0, 2)):
+        for o in pair:
+            for sign in SIGNS:
+                c_copies[o, sign, 2].wait_recv()
+                if far(o, sign):
+                    c_copies[o, sign, 3].wait_recv()
+        k = (yi + pair[0]) % STEPS
+        last.append((k, compute((3, -3, 4), k)))
+    for k, copies in last:
+        forward((3, -3, 4), copies, (k,))
+
     for k in range(STEPS):
+        total = half[(qi + NQ // 2 * k) % NQ, k].astype(jnp.float32)
+        for away in range(1, NQ):
+            h_copy(away, 0, k).wait_recv()
+            total += land_h[away - 1, k].astype(jnp.float32)
         upper = blk >= owner_ref[k]
-        out_ref[k] = jnp.where(upper, total[k], 0.0)
-
-    for copies in (a_copies, b_copies, g_copies, c_copies, e_copies):
+        out_ref[k] = jnp.where(upper, total, 0.0)
+
+    for copy in near + next_one + next_two + last[0][1] + last[1][1]:
+        copy.wait_send()
+    for away in range(1, NQ):
+        for k in range(STEPS):
+            h_copy(away, 0, k).wait_send()
+    for copies in (a_copies, b_copies, g_copies, c_copies):
         for copy in copies.values():
             copy.wait_send()
-    for o in range(1, NQ):
-        h_copy(o, (qi + o) % NQ).wait_send()
 
 
 def body(series, labels, panel_owner):
@@ -327,7 +348,7 @@
             pltpu.VMEM((NQ, STEPS, OUT_ROWS, COLUMNS), half_type),
             pltpu.VMEM((NQ, STEPS, OUT_ROWS, COLUMNS), half_type),
             pltpu.VMEM((NQ - 1, STEPS, OUT_ROWS, COLUMNS), half_type),
-            pltpu.SemaphoreType.DMA((5,)),
+            pltpu.SemaphoreType.DMA((NY + 3,)),
             pltpu.SemaphoreType.DMA((N_COPIES,)),
             pltpu.SemaphoreType.DMA((N_COPIES,)),
         ],

time: 67.1 us -> 64.9 us (0.967)
  the two profiles are of different devices: /device:TPU:12 before, /device:TPU:1 now
where the time goes in v5:
time: 64.9 us; the launch traced here: 64.7 us
  Pallas kernels  63.1 us (97%)
  other arithmetic  1.58 us (2%)
    pallas_call x1, Pallas kernels, body(): pl.pallas_call(kernel, out_shape=jax.ShapeDtypeStruct((STEPS, OUT_ROWS, C...  63.1 us
    convert_element_type x1, other arithmetic, body(): return summed.astype(half_type)  1.58 us

profile of v5, /device:TPU:1, one launch (start us, length us, event | category | flops | bytes accessed | tf_op | source)
XLA Modules:
  0.0 64.7 jit_solution(7805768056719676655)
XLA Ops:
  0.0 63.1 %shard_map.37 = f32[2,16,1536]{2,1,0:T(8,128)} custom-call(s32[32]{0:T(128)} %labels_hbm.1, s32[2]{0:T(128)} %owner_hbm.1, bf16[2,512,1536]{2,1,0:T(8,128)(2,1)} %series_ref.1), custom_call_target="tpu_custom_call" | custom-call | tf_op jit(solution)/shard_map/pallas_call | solution.py:332
  63.1 1.6 %convert_element_type.3 = bf16[2,16,1536]{2,1,0:T(8,128)(2,1)} convert(f32[2,16,1536]{2,1,0:T(8,128)} %shard_map.37) | non-fusion elementwise | flops 49152 | bytes 294912 | tf_op jit(solution)/shard_map/convert_element_type | solution.py:359

commit v6 on v5

--- a/solution.py
+++ b/solution.py
@@ -134,25 +134,37 @@
     SIGNS = (1, -1)
     a_copies = {}
 
-    def send_a(o, sign, t):
-        way = 0 if sign > 0 else 1
-        j = (yi + o) % NY
-        mine = panel.at[(zi + sign * (3 - t) + NZ) % NZ, j]
-        if t == 0:
+    def side(o, sign, slot):
+        return land_a.at[o, 0 if sign > 0 else 1, slot]
+
+    def own(o, offset):
+        return panel.at[(zi + offset + NZ) % NZ, (yi + o) % NY]
+
+    def send_outer(o):
+        for sign in SIGNS:
             if far(o, sign):
                 a_copies[o, sign, 3] = send(
-                    panel.at[(zi + 4) % NZ, j], land_a.at[o, way, 3], at_z(2 * sign)
+                    own(o, 4), side(o, sign, 3), at_z(2 * sign)
                 )
-            src = mine
-        else:
-            a_copies[o, sign, t - 1].wait_recv()
-            src = land_a.at[o, way, t - 1]
-            if t == 1 and far(o, sign):
+        for sign in SIGNS:
+            a_copies[o, sign, 0] = send(
+                own(o, 3 * sign), side(o, sign, 0), at_z(sign)
+            )
+
+    def send_next(o):
+        for sign in SIGNS:
+            a_copies[o, sign, 1] = send(own(o, sign), side(o, sign, 1), at_z(sign))
+
+    def send_sum(o):
+        for sign in SIGNS:
+            a_copies[o, sign, 0].wait_recv()
+            src = side(o, sign, 0)
+            if far(o, sign):
                 a_copies[o, sign, 3].wait_recv()
-                src[...] += mine[...] + land_a[o, way, 3]
+                src[...] += own(o, 2 * sign)[...] + side(o, sign, 3)[...]
             else:
-                src[...] += mine[...]
-        a_copies[o, sign, t] = send(src, land_a.at[o, way, t], at_z(sign))
+                src[...] += own(o, 2 * sign)[...]
+            a_copies[o, sign, 2] = send(src, side(o, sign, 2), at_z(2 * sign))
 
     small[0].wait()
     for i, o in enumerate(order):
@@ -161,21 +173,23 @@
         standardize(s, k * PANEL, k)
         if i == 0:
             pl.semaphore_wait(barrier, len(peers))
-        for sign in SIGNS:
-            send_a(o, sign, 0)
+        send_outer(o)
+    for o in order:
+        send_next(o)
     loads[NY].wait()
     some_rest(4)
-    for t in range(1, 3):
-        for o in order:
-            for sign in SIGNS:
-                send_a(o, sign, t)
-        some_rest(2)
+    for o in order:
+        send_sum(o)
+    some_rest(4)
 
     b_copies = {}
     for o in order:
-        for sign in SIGNS:
-            a_copies[o, sign, 2].wait_recv()
-        mid[o] = panel[zi, (yi + o) % NY] + land_a[o, 0, 2] + land_a[o, 1, 2]
+        total = own(o, 0)[...]
+        for sign in SIGNS:
+            for slot in (1, 2):
+                a_copies[o, sign, slot].wait_recv()
+                total += side(o, sign, slot)[...]
+        mid[o] = total
         if o:
             b_copies[o] = send(mid.at[o], land_b.at[o - 1], at_y(o))
     for o in (1, 3, 2):
@@ -274,28 +288,41 @@
                 def _():
                     h_copy(away, d, k).start()
 
-    def hop(o, t):
-        if t == 0:
-            g_copies[o].wait_recv()
-        for sign in SIGNS:
-            send_c(o, sign, t)
-
-    hop(1, 0)
-    hop(3, 0)
-    hop(0, 1)
-    hop(2, 0)
+    def hop(t):
+        for sign in SIGNS:
+            send_c(0, sign, t)
+
+    def spread(o):
+        g_copies[o].wait_recv()
+        piece = whole.at[zi, (yi - o + NY) % NY]
+        for t in (1, 0):
+            for sign in SIGNS:
+                c_copies[o, sign, t] = send(piece, piece, at_z((t + 1) * sign))
+
+    def spread_on(o):
+        for sign in SIGNS:
+            c_copies[o, sign, 1].wait_recv()
+            piece = whole.at[(zi - 2 * sign + NZ) % NZ, (yi - o + NY) % NY]
+            if far(o, sign):
+                c_copies[o, sign, 3] = send(piece, piece, at_z(2 * sign))
+            c_copies[o, sign, 2] = send(piece, piece, at_z(sign))
+
+    spread(1)
+    spread(3)
+    hop(1)
+    spread(2)
     near = compute((0,))
-    hop(1, 1)
-    hop(3, 1)
-    hop(0, 2)
-    hop(2, 1)
+    hop(2)
+    spread_on(1)
+    spread_on(3)
+    spread_on(2)
     forward((0,), near)
+    for o in (1, 3, 2):
+        for sign in SIGNS:
+            c_copies[o, sign, 0].wait_recv()
     next_one = compute((1, -1))
-    hop(1, 2)
-    hop(3, 2)
-    hop(2, 2)
+    next_two = compute((2, -2))
     forward((1, -1), next_one)
-    next_two = compute((2, -2))
     forward((2, -2), next_two)
     last = []
     for pair in ((1, 3), (0, 2)):

time: 64.9 us -> 66 us (1.017)
  Pallas kernels: 63.1 us -> 64.3 us
    pallas_call x1, Pallas kernels: 63.1 us -> 64.3 us  [body(): pl.pallas_call(kernel, out_shape=jax.ShapeDtypeStruct((STEPS, OUT_ROWS, C...]
where the time goes in v6:
time: 66 us; the launch traced here: 65.9 us
  Pallas kernels  64.3 us (97%)
  other arithmetic  1.58 us (2%)
    pallas_call x1, Pallas kernels, body(): pl.pallas_call(kernel, out_shape=jax.ShapeDtypeStruct((STEPS, OUT_ROWS, C...  64.3 us
    convert_element_type x1, other arithmetic, body(): return summed.astype(half_type)  1.58 us

profile of v6, /device:TPU:1, one launch (start us, length us, event | category | flops | bytes accessed | tf_op | source)
XLA Modules:
  0.0 65.9 jit_solution(8243454523575971112)
XLA Ops:
  0.0 64.3 %shard_map.37 = f32[2,16,1536]{2,1,0:T(8,128)} custom-call(s32[32]{0:T(128)} %labels_hbm.1, s32[2]{0:T(128)} %owner_hbm.1, bf16[2,512,1536]{2,1,0:T(8,128)(2,1)} %series_ref.1), custom_call_target="tpu_custom_call" | custom-call | tf_op jit(solution)/shard_map/pallas_call | solution.py:359
  64.3 1.6 %convert_element_type.3 = bf16[2,16,1536]{2,1,0:T(8,128)(2,1)} convert(f32[2,16,1536]{2,1,0:T(8,128)} %shard_map.37) | non-fusion elementwise | flops 49152 | bytes 294912 | tf_op jit(solution)/shard_map/convert_element_type | solution.py:386

commit v7 on v5

--- a/solution.py
+++ b/solution.py
@@ -154,6 +154,10 @@
                 src[...] += mine[...]
         a_copies[o, sign, t] = send(src, land_a.at[o, way, t], at_z(sign))
 
+    def step_a(o, t):
+        for sign in SIGNS:
+            send_a(o, sign, t)
+
     small[0].wait()
     for i, o in enumerate(order):
         loads[i].wait()
@@ -161,18 +165,24 @@
         standardize(s, k * PANEL, k)
         if i == 0:
             pl.semaphore_wait(barrier, len(peers))
-        for sign in SIGNS:
-            send_a(o, sign, 0)
+        if o:
+            step_a(o, 0)
     loads[NY].wait()
     some_rest(4)
-    for t in range(1, 3):
-        for o in order:
-            for sign in SIGNS:
-                send_a(o, sign, t)
-        some_rest(2)
+    step_a(2, 1)
+    step_a(0, 0)
+    step_a(1, 1)
+    step_a(3, 1)
+    some_rest(4)
+    step_a(2, 2)
+    step_a(0, 1)
+    step_a(1, 2)
+    step_a(3, 2)
 
     b_copies = {}
     for o in order:
+        if o == 1:
+            step_a(0, 2)
         for sign in SIGNS:
             a_copies[o, sign, 2].wait_recv()
         mid[o] = panel[zi, (yi + o) % NY] + land_a[o, 0, 2] + land_a[o, 1, 2]

time: 64.9 us -> 65.1 us (level)
  no operation moved by 1% of the time
where the time goes in v7:
time: 65.1 us; the launch traced here: 64.9 us
  Pallas kernels  63.4 us (97%)
  other arithmetic  1.58 us (2%)
    pallas_call x1, Pallas kernels, body(): pl.pallas_call(kernel, out_shape=jax.ShapeDtypeStruct((STEPS, OUT_ROWS, C...  63.4 us
    convert_element_type x1, other arithmetic, body(): return summed.astype(half_type)  1.58 us

profile of v7, /device:TPU:1, one launch (start us, length us, event | category | flops | bytes accessed | tf_op | source)
XLA Modules:
  0.0 64.9 jit_solution(11420584926225149178)
XLA Ops:
  0.0 63.4 %shard_map.37 = f32[2,16,1536]{2,1,0:T(8,128)} custom-call(s32[32]{0:T(128)} %labels_hbm.1, s32[2]{0:T(128)} %owner_hbm.1, bf16[2,512,1536]{2,1,0:T(8,128)(2,1)} %series_ref.1), custom_call_target="tpu_custom_call" | custom-call | tf_op jit(solution)/shard_map/pallas_call | solution.py:342
  63.4 1.6 %convert_element_type.3 = bf16[2,16,1536]{2,1,0:T(8,128)(2,1)} convert(f32[2,16,1536]{2,1,0:T(8,128)} %shard_map.37) | non-fusion elementwise | flops 49152 | bytes 294912 | tf_op jit(solution)/shard_map/convert_element_type | solution.py:369

commit v8 on v7

--- a/solution.py
+++ b/solution.py
@@ -20,12 +20,12 @@
 epsilon = 1e-05
 clip_limit = 0.99
 
-N_COPIES = NY * (7 + 7) + 6 + NQ + 3 + STEPS * (NQ - 1)
+N_COPIES = NY * (7 + 7) + 2 * NY + NQ + 3 + STEPS * NQ
 
 
 def kernel(
     labels_hbm, owner_hbm, series_ref, out_ref,
-    labels_ref, owner_ref, raw, scored, panel, land_a, mid, land_b, whole,
+    labels_ref, owner_ref, raw, scored, panel, land_a, mid, land_b, found, whole,
     part, land_e, half, land_h, load_sem, send_sem, recv_sem,
 ):
     grp, blk = lax.axis_index("grp"), lax.axis_index("blk")
@@ -36,12 +36,20 @@
         return {"blk": ((zi + offset + NZ) % NZ) * NY + yi}
 
     def at_y(offset):
-        return {"blk": zi * NY + (yi + offset) % NY}
+        return {"grp": qi * NC + 1 - core, "blk": zi * NY + (yi + offset) % NY}
 
     def at_q(offset):
-        return {"grp": ((qi + offset) % NQ) * NC + core}
-
-    other_core = {"grp": qi * NC + 1 - core}
+        return {"grp": ((qi + offset) % NQ) * NC + 1 - core}
+
+    other_core = at_q(0)
+
+    barrier = pltpu.get_barrier_semaphore()
+    peers = [at_y(o) for o in (2, 1, 3)]
+    peers += [at_z(o) for o in (1, -1, 2, -2)]
+    peers += [at_q(o) for o in range(1, NQ)]
+    peers += [other_core]
+    for peer in peers:
+        pl.semaphore_signal(barrier, inc=1, device_id=peer, device_id_type=MESH)
 
     loads = []
     small = [
@@ -67,14 +75,6 @@
         )
     )
     loads[-1].start()
-
-    barrier = pltpu.get_barrier_semaphore()
-    peers = [at_y(o) for o in (2, 1, 3)]
-    peers += [at_z(o) for o in (1, -1, 2, -2)]
-    peers += [at_q(o) for o in range(1, NQ)]
-    peers += [other_core]
-    for peer in peers:
-        pl.semaphore_signal(barrier, inc=1, device_id=peer, device_id_type=MESH)
 
     count = [0]
 
@@ -186,11 +186,10 @@
         for sign in SIGNS:
             a_copies[o, sign, 2].wait_recv()
         mid[o] = panel[zi, (yi + o) % NY] + land_a[o, 0, 2] + land_a[o, 1, 2]
-        if o:
-            b_copies[o] = send(mid.at[o], land_b.at[o - 1], at_y(o))
-    for o in (1, 3, 2):
+        b_copies[o] = send(mid.at[o], land_b.at[o], at_y(o))
+    for o in (1, 3, 2, 0):
         b_copies[o].wait_recv()
-    whole[zi, yi] = mid[0] + land_b[0] + land_b[1] + land_b[2]
+    found[...] = land_b[0] + land_b[1] + land_b[2] + land_b[3]
     g_copies, c_copies = {}, {}
 
     def send_c(o, sign, t):
@@ -201,8 +200,9 @@
             c_copies[o, sign, 3] = send(piece, piece, at_z(2 * sign))
         c_copies[o, sign, t] = send(piece, piece, at_z(sign))
 
-    for o in (2, 1, 3):
-        g_copies[o] = send(whole.at[zi, yi], whole.at[zi, yi], at_y(o))
+    for o in order:
+        g_copies[o] = send(found, whole.at[zi, yi], at_y(o))
+    g_copies[0].wait_recv()
     for sign in SIGNS:
         send_c(0, sign, 0)
 
@@ -251,18 +251,18 @@
         lax.fori_loop(0, COLUMNS // WIDE, tile, 0)
         mine = pl.ds(first, steps)
         return [
-            send(part.at[d, 1 - core, mine], land_e.at[d, mine], other_core)
+            send(part.at[d, core, mine], land_e.at[d, mine], other_core)
             for d in chunks
         ]
 
     base = count[0]
-    count[0] += STEPS * (NQ - 1)
+    count[0] += STEPS * NQ
 
     def h_copy(away, d, k):
-        at = base + (away - 1) * STEPS + k
+        at = base + away * STEPS + k
         return pltpu.make_async_remote_copy(
             src_ref=half.at[d, k],
-            dst_ref=land_h.at[away - 1, k],
+            dst_ref=land_h.at[away, k],
             send_sem=send_sem.at[at],
             recv_sem=recv_sem.at[at],
             device_id=at_q(away),
@@ -275,14 +275,10 @@
             copy.wait_recv()
             for k in steps:
                 half[d, k] = (
-                    part[d, core, k].astype(jnp.float32)
+                    part[d, 1 - core, k].astype(jnp.float32)
                     + land_e[d, k].astype(jnp.float32)
                 ).astype(jnp.bfloat16)
-                away = (d + NQ // 2 * k - qi + NQ) % NQ
-
-                @pl.when(away != 0)
-                def _():
-                    h_copy(away, d, k).start()
+                h_copy((d + NQ // 2 * k - qi + NQ) % NQ, d, k).start()
 
     def hop(o, t):
         if t == 0:
@@ -320,16 +316,17 @@
         forward((3, -3, 4), copies, (k,))
 
     for k in range(STEPS):
-        total = half[(qi + NQ // 2 * k) % NQ, k].astype(jnp.float32)
-        for away in range(1, NQ):
+        total = None
+        for away in range(NQ):
             h_copy(away, 0, k).wait_recv()
-            total += land_h[away - 1, k].astype(jnp.float32)
+            term = land_h[away, k].astype(jnp.float32)
+            total = term if total is None else total + term
         upper = blk >= owner_ref[k]
         out_ref[k] = jnp.where(upper, total, 0.0)
 
     for copy in near + next_one + next_two + last[0][1] + last[1][1]:
         copy.wait_send()
-    for away in range(1, NQ):
+    for away in range(NQ):
         for k in range(STEPS):
             h_copy(away, 0, k).wait_send()
     for copies in (a_copies, b_copies, g_copies, c_copies):
@@ -352,12 +349,13 @@
             pltpu.VMEM((NZ, NY, PIECE, FRAMES), half_type),
             pltpu.VMEM((NY, 2, 4, PIECE, FRAMES), half_type),
             pltpu.VMEM((NY, PIECE, FRAMES), half_type),
-            pltpu.VMEM((NY - 1, PIECE, FRAMES), half_type),
+            pltpu.VMEM((NY, PIECE, FRAMES), half_type),
+            pltpu.VMEM((PIECE, FRAMES), half_type),
             pltpu.VMEM((NZ, NY, PIECE, FRAMES), half_type),
             pltpu.VMEM((NQ, NC, STEPS, OUT_ROWS, COLUMNS), half_type),
             pltpu.VMEM((NQ, STEPS, OUT_ROWS, COLUMNS), half_type),
             pltpu.VMEM((NQ, STEPS, OUT_ROWS, COLUMNS), half_type),
-            pltpu.VMEM((NQ - 1, STEPS, OUT_ROWS, COLUMNS), half_type),
+            pltpu.VMEM((NQ, STEPS, OUT_ROWS, COLUMNS), half_type),
             pltpu.SemaphoreType.DMA((NY + 3,)),
             pltpu.SemaphoreType.DMA((N_COPIES,)),
             pltpu.SemaphoreType.DMA((N_COPIES,)),

time: 65.1 us -> 64.5 us (level)
  Pallas kernels: 63.4 us -> 62.5 us
    pallas_call x1, Pallas kernels: 63.4 us -> 62.5 us  [body(): pl.pallas_call(kernel, out_shape=jax.ShapeDtypeStruct((STEPS, OUT_ROWS, C...]
where the time goes in v8:
time: 64.5 us; the launch traced here: 64.1 us
  Pallas kernels  62.5 us (97%)
  other arithmetic  1.58 us (2%)
    pallas_call x1, Pallas kernels, body(): pl.pallas_call(kernel, out_shape=jax.ShapeDtypeStruct((STEPS, OUT_ROWS, C...  62.5 us
    convert_element_type x1, other arithmetic, body(): return summed.astype(half_type)  1.58 us

profile of v8, /device:TPU:1, one launch (start us, length us, event | category | flops | bytes accessed | tf_op | source)
XLA Modules:
  0.0 64.1 jit_solution(8776183348343643264)
XLA Ops:
  0.0 62.5 %shard_map.37 = f32[2,16,1536]{2,1,0:T(8,128)} custom-call(s32[32]{0:T(128)} %labels_hbm.1, s32[2]{0:T(128)} %owner_hbm.1, bf16[2,512,1536]{2,1,0:T(8,128)(2,1)} %series_ref.1), custom_call_target="tpu_custom_call" | custom-call | tf_op jit(solution)/shard_map/pallas_call | solution.py:339
  62.5 1.6 %convert_element_type.3 = bf16[2,16,1536]{2,1,0:T(8,128)(2,1)} convert(f32[2,16,1536]{2,1,0:T(8,128)} %shard_map.37) | non-fusion elementwise | flops 49152 | bytes 294912 | tf_op jit(solution)/shard_map/convert_element_type | solution.py:367

commit v9 on v8

--- a/solution.py
+++ b/solution.py
@@ -296,9 +296,9 @@
     hop(0, 2)
     hop(2, 1)
     forward((0,), near)
-    next_one = compute((1, -1))
     hop(1, 2)
     hop(3, 2)
+    next_one = compute((1, -1))
     hop(2, 2)
     forward((1, -1), next_one)
     next_two = compute((2, -2))
@@ -315,6 +315,15 @@
     for k, copies in last:
         forward((3, -3, 4), copies, (k,))
 
+    for copy in near + next_one + next_two + last[0][1] + last[1][1]:
+        copy.wait_send()
+    for away in range(NQ):
+        for k in range(STEPS):
+            h_copy(away, 0, k).wait_send()
+    for copies in (a_copies, b_copies, g_copies, c_copies):
+        for copy in copies.values():
+            copy.wait_send()
+
     for k in range(STEPS):
         total = None
         for away in range(NQ):
@@ -323,15 +332,6 @@
             total = term if total is None else total + term
         upper = blk >= owner_ref[k]
         out_ref[k] = jnp.where(upper, total, 0.0)
-
-    for copy in near + next_one + next_two + last[0][1] + last[1][1]:
-        copy.wait_send()
-    for away in range(NQ):
-        for k in range(STEPS):
-            h_copy(away, 0, k).wait_send()
-    for copies in (a_copies, b_copies, g_copies, c_copies):
-        for copy in copies.values():
-            copy.wait_send()
 
 
 def body(series, labels, panel_owner):

time: 64.5 us -> 65.3 us (1.012)
  Pallas kernels: 62.5 us -> 63.6 us
    pallas_call x1, Pallas kernels: 62.5 us -> 63.6 us  [body(): pl.pallas_call(kernel, out_shape=jax.ShapeDtypeStruct((STEPS, OUT_ROWS, C...]
where the time goes in v9:
time: 65.3 us; the launch traced here: 65.2 us
  Pallas kernels  63.6 us (97%)
  other arithmetic  1.58 us (2%)
    pallas_call x1, Pallas kernels, body(): pl.pallas_call(kernel, out_shape=jax.ShapeDtypeStruct((STEPS, OUT_ROWS, C...  63.6 us
    convert_element_type x1, other arithmetic, body(): return summed.astype(half_type)  1.58 us

profile of v9, /device:TPU:1, one launch (start us, length us, event | category | flops | bytes accessed | tf_op | source)
XLA Modules:
  0.0 65.2 jit_solution(1618078897897295092)
XLA Ops:
  0.0 63.6 %shard_map.37 = f32[2,16,1536]{2,1,0:T(8,128)} custom-call(s32[32]{0:T(128)} %labels_hbm.1, s32[2]{0:T(128)} %owner_hbm.1, bf16[2,512,1536]{2,1,0:T(8,128)(2,1)} %series_ref.1), custom_call_target="tpu_custom_call" | custom-call | tf_op jit(solution)/shard_map/pallas_call | solution.py:339
  63.6 1.6 %convert_element_type.3 = bf16[2,16,1536]{2,1,0:T(8,128)(2,1)} convert(f32[2,16,1536]{2,1,0:T(8,128)} %shard_map.37) | non-fusion elementwise | flops 49152 | bytes 294912 | tf_op jit(solution)/shard_map/convert_element_type | solution.py:367

commit v10 on v9

--- a/solution.py
+++ b/solution.py
@@ -296,9 +296,9 @@
     hop(0, 2)
     hop(2, 1)
     forward((0,), near)
+    next_one = compute((1, -1))
     hop(1, 2)
     hop(3, 2)
-    next_one = compute((1, -1))
     hop(2, 2)
     forward((1, -1), next_one)
     next_two = compute((2, -2))
@@ -331,14 +331,14 @@
             term = land_h[away, k].astype(jnp.float32)
             total = term if total is None else total + term
         upper = blk >= owner_ref[k]
-        out_ref[k] = jnp.where(upper, total, 0.0)
+        out_ref[k] = jnp.where(upper, total, 0.0).astype(out_ref.dtype)
 
 
 def body(series, labels, panel_owner):
     half_type = jnp.bfloat16
-    summed = pl.pallas_call(
+    return pl.pallas_call(
         kernel,
-        out_shape=jax.ShapeDtypeStruct((STEPS, OUT_ROWS, COLUMNS), jnp.float32),
+        out_shape=jax.ShapeDtypeStruct((STEPS, OUT_ROWS, COLUMNS), half_type),
         in_specs=[pl.BlockSpec(memory_space=pltpu.HBM)] * 3,
         out_specs=pl.BlockSpec(memory_space=pltpu.VMEM),
         scratch_shapes=[
@@ -364,7 +364,6 @@
             collective_id=0, has_side_effects=True, vmem_limit_bytes=60 * 1024 * 1024
         ),
     )(labels, panel_owner, series)
-    return summed.astype(half_type)
 
 
 def solution(mesh):

time: 65.3 us -> 64.2 us (0.983)
  other arithmetic: 1.58 us -> 0 us
  local copies, waits for them, and re-layouts: 0 us -> 1.54 us
  Pallas kernels: 63.6 us -> 62.3 us
    convert_element_type x1 -> x0, other arithmetic: 1.58 us -> none  [body(): return summed.astype(half_type)]
    unnamed x0 -> x1, local copies, waits for them, and re-layouts: none -> 1.54 us
    pallas_call x1, Pallas kernels: 63.6 us -> 62.3 us  [body(): pl.pallas_call(kernel, out_shape=jax.ShapeDtypeStruct((STEPS, OUT_ROWS, C...]
where the time goes in v10:
time: 64.2 us; the launch traced here: 63.8 us
  Pallas kernels  62.3 us (97%)
  local copies, waits for them, and re-layouts  1.54 us (2%)
    pallas_call x1, Pallas kernels, body(): pl.pallas_call(kernel, out_shape=jax.ShapeDtypeStruct((STEPS, OUT_ROWS, C...  62.3 us
    unnamed x1, local copies, waits for them, and re-layouts  1.54 us

profile of v10, /device:TPU:1, one launch (start us, length us, event | category | flops | bytes accessed | tf_op | source)
XLA Modules:
  0.0 63.8 jit_solution(9655478478333041324)
XLA Ops:
  0.0 62.3 %shard_map.37 = bf16[2,16,1536]{2,1,0:T(8,128)(2,1)} custom-call(s32[32]{0:T(128)} %labels_hbm.1, s32[2]{0:T(128)} %owner_hbm.1, bf16[2,512,1536]{2,1,0:T(8,128)(2,1)} %series_ref.1), custom_call_target="tpu_custom_call" | custom-call | tf_op jit(solution)/shard_map/pallas_call | solution.py:339
  62.3 1.5 %copy.5 = bf16[2,16,1536]{2,1,0:T(8,128)(2,1)} copy(bf16[2,16,1536]{2,1,0:T(8,128)(2,1)} %shard_map.37) | data formatting | bytes 196608

commit v11 on v10

--- a/solution.py
+++ b/solution.py
@@ -15,7 +15,7 @@
 PIECE = PANEL // NZ
 OUT_ROWS = PANEL // N_GRP
 TILE = 256
-WIDE = 512
+WIDE = 768
 ROWS = 128
 epsilon = 1e-05
 clip_limit = 0.99
@@ -134,12 +134,16 @@
     SIGNS = (1, -1)
     a_copies = {}
 
+    def reach(o, sign):
+        return 4 if o == 0 and far(o, sign) else 3
+
     def send_a(o, sign, t):
         way = 0 if sign > 0 else 1
         j = (yi + o) % NY
-        mine = panel.at[(zi + sign * (3 - t) + NZ) % NZ, j]
+        mine = panel.at[(zi + sign * (reach(o, sign) - t) + NZ) % NZ, j]
+        jump = o != 0 and far(o, sign)
         if t == 0:
-            if far(o, sign):
+            if jump:
                 a_copies[o, sign, 3] = send(
                     panel.at[(zi + 4) % NZ, j], land_a.at[o, way, 3], at_z(2 * sign)
                 )
@@ -147,7 +151,7 @@
         else:
             a_copies[o, sign, t - 1].wait_recv()
             src = land_a.at[o, way, t - 1]
-            if t == 1 and far(o, sign):
+            if t == 1 and jump:
                 a_copies[o, sign, 3].wait_recv()
                 src[...] += mine[...] + land_a[o, way, 3]
             else:
@@ -183,9 +187,16 @@
     for o in order:
         if o == 1:
             step_a(0, 2)
-        for sign in SIGNS:
-            a_copies[o, sign, 2].wait_recv()
-        mid[o] = panel[zi, (yi + o) % NY] + land_a[o, 0, 2] + land_a[o, 1, 2]
+        if o == 0:
+            for sign in SIGNS:
+                if far(0, sign):
+                    send_a(0, sign, 3)
+        total = panel[zi, (yi + o) % NY]
+        for way, sign in enumerate(SIGNS):
+            t = reach(o, sign) - 1
+            a_copies[o, sign, t].wait_recv()
+            total += land_a[o, way, t]
+        mid[o] = total
         b_copies[o] = send(mid.at[o], land_b.at[o], at_y(o))
     for o in (1, 3, 2, 0):
         b_copies[o].wait_recv()
@@ -196,7 +207,7 @@
         if t:
             c_copies[o, sign, t - 1].wait_recv()
         piece = whole.at[(zi - sign * t + NZ) % NZ, (yi - o + NY) % NY]
-        if t == 2 and far(o, sign):
+        if o and t == 2 and far(o, sign):
             c_copies[o, sign, 3] = send(piece, piece, at_z(2 * sign))
         c_copies[o, sign, t] = send(piece, piece, at_z(sign))
 
@@ -302,12 +313,16 @@
     hop(2, 2)
     forward((1, -1), next_one)
     next_two = compute((2, -2))
+    for sign in SIGNS:
+        if far(0, sign):
+            send_c(0, sign, 3)
     forward((2, -2), next_two)
     last = []
     for pair in ((1, 3), (0, 2)):
         for o in pair:
             for sign in SIGNS:
-                c_copies[o, sign, 2].wait_recv()
+                if reach(o, sign) == 3:
+                    c_copies[o, sign, 2].wait_recv()
                 if far(o, sign):
                     c_copies[o, sign, 3].wait_recv()
         k = (yi + pair[0]) % STEPS

time: 64.2 us -> 64.3 us (level)
  no operation moved by 1% of the time
where the time goes in v11:
time: 64.3 us; the launch traced here: 64.1 us
  Pallas kernels  62.5 us (97%)
  local copies, waits for them, and re-layouts  1.54 us (2%)
    pallas_call x1, Pallas kernels, body(): pl.pallas_call(kernel, out_shape=jax.ShapeDtypeStruct((STEPS, OUT_ROWS, C...  62.5 us
    unnamed x1, local copies, waits for them, and re-layouts  1.54 us

profile of v11, /device:TPU:1, one launch (start us, length us, event | category | flops | bytes accessed | tf_op | source)
XLA Modules:
  0.0 64.1 jit_solution(3184842751667658735)
XLA Ops:
  0.0 62.5 %shard_map.37 = bf16[2,16,1536]{2,1,0:T(8,128)(2,1)} custom-call(s32[32]{0:T(128)} %labels_hbm.1, s32[2]{0:T(128)} %owner_hbm.1, bf16[2,512,1536]{2,1,0:T(8,128)(2,1)} %series_ref.1), custom_call_target="tpu_custom_call" | custom-call | tf_op jit(solution)/shard_map/pallas_call | solution.py:354
  62.5 1.5 %copy.5 = bf16[2,16,1536]{2,1,0:T(8,128)(2,1)} copy(bf16[2,16,1536]{2,1,0:T(8,128)(2,1)} %shard_map.37) | data formatting | bytes 196608

commit v12 on v10

--- a/solution.py
+++ b/solution.py
@@ -15,7 +15,7 @@
 PIECE = PANEL // NZ
 OUT_ROWS = PANEL // N_GRP
 TILE = 256
-WIDE = 512
+WIDE = 768
 ROWS = 128
 epsilon = 1e-05
 clip_limit = 0.99
@@ -48,16 +48,19 @@
     peers += [at_z(o) for o in (1, -1, 2, -2)]
     peers += [at_q(o) for o in range(1, NQ)]
     peers += [other_core]
-    for peer in peers:
-        pl.semaphore_signal(barrier, inc=1, device_id=peer, device_id_type=MESH)
+
+    def greet(some):
+        for peer in some:
+            pl.semaphore_signal(barrier, inc=1, device_id=peer, device_id_type=MESH)
+
+    greet(peers[:7])
 
     loads = []
     small = [
         pltpu.make_async_copy(owner_hbm, owner_ref, load_sem.at[NY + 1]),
         pltpu.make_async_copy(labels_hbm, labels_ref, load_sem.at[NY + 2]),
     ]
-    for copy in small:
-        copy.start()
+    small[0].start()
     order = (2, 1, 3, 0)
     for i, o in enumerate(order):
         s, k = (yi + o) % NY // STEPS, (yi + o) % STEPS
@@ -68,6 +71,9 @@
             )
         )
         loads[-1].start()
+        if i == 0:
+            greet(peers[7:])
+    small[1].start()
     cols = pl.ds(STEPS * PANEL, COLUMNS - STEPS * PANEL)
     loads.append(
         pltpu.make_async_copy(

time: 64.2 us -> 63.7 us (level)
  no operation moved by 1% of the time
where the time goes in v12:
time: 63.7 us; the launch traced here: 63.4 us
  Pallas kernels  61.8 us (97%)
  local copies, waits for them, and re-layouts  1.54 us (2%)
    pallas_call x1, Pallas kernels, body(): pl.pallas_call(kernel, out_shape=jax.ShapeDtypeStruct((STEPS, OUT_ROWS, C...  61.8 us
    unnamed x1, local copies, waits for them, and re-layouts  1.54 us

profile of v12, /device:TPU:1, one launch (start us, length us, event | category | flops | bytes accessed | tf_op | source)
XLA Modules:
  0.0 63.4 jit_solution(16215551772812105666)
XLA Ops:
  0.0 61.8 %shard_map.37 = bf16[2,16,1536]{2,1,0:T(8,128)(2,1)} custom-call(s32[32]{0:T(128)} %labels_hbm.1, s32[2]{0:T(128)} %owner_hbm.1, bf16[2,512,1536]{2,1,0:T(8,128)(2,1)} %series_ref.1), custom_call_target="tpu_custom_call" | custom-call | tf_op jit(solution)/shard_map/pallas_call | solution.py:345
  61.9 1.5 %copy.5 = bf16[2,16,1536]{2,1,0:T(8,128)(2,1)} copy(bf16[2,16,1536]{2,1,0:T(8,128)(2,1)} %shard_map.37) | data formatting | bytes 196608
